TPU v7x, 512 devices: a whole 4x4x16 slice. The times are simulated.
512 devices in a mesh: replica: 32 (over z, core), fsdp: 16 (over y, x).
Axes of the slice: x: 4, y: 4, z: 16, core: 2. Of those that a mesh axis runs over, the one named last changes fastest.
Arguments:
- weights: bfloat16 [3, 32, 28672], P(None, None, 'fsdp'), may hold values from -4 to 4
- local_weights: bfloat16 [32, 3, 32, 28672], P('replica', None, None, 'fsdp'), may hold values from -11 to 11
- carried_error: float32 [32, 3, 32, 28672], P('replica', None, None, 'fsdp'), may hold values from -4 to 4
- momentum: float32 [3, 32, 28672], P(None, None, 'fsdp'), may hold values from -4 to 4
- initial_factor: float32 [3, 32, 16], replicated, may hold values from -5 to 5
Outputs:
- next_weights: bfloat16 [3, 32, 28672], P(None, None, 'fsdp')
- next_error: float32 [32, 3, 32, 28672], P('replica', None, None, 'fsdp')
- next_momentum: float32 [3, 32, 28672], P(None, None, 'fsdp')
- following_factor: float32 [3, 32, 16], replicated
All inputs are finite; a program needn't handle non-finite values.
Results may differ from a plain program's by a relative error of at most 0.001.
Values sent between devices are 32-bit elements; how exact they have to be, the bound alone decides.
No kernel may reach another device: no remote copies, remote signals or barrier semaphores. Data moves between devices by JAX's collectives and lax.ppermute only.
A program may use at most 64 MiB of HBM per device.

v0:
```python
import jax
import jax.numpy as jnp
from jax import lax
from jax.experimental import pallas as pl
from jax.experimental.pallas import tpu as pltpu
from jax.sharding import PartitionSpec as P

CHIPS = 16
BLOCK = 128
SIDE = BLOCK // 2
BLOCKS = 14
WIDTH = BLOCK * BLOCKS
MATS = 3
COLS = 32
RANK = 16
SHARE = MATS * COLS // 2
FROWS = SHARE // 2
MROWS = 8
GROWS = FROWS + MROWS
PAIR = RANK + COLS
HIGHEST = lax.Precision.HIGHEST
VMEM = pl.BlockSpec(memory_space=pltpu.VMEM)
SMEM = pl.BlockSpec(memory_space=pltpu.SMEM)
HBM = pl.BlockSpec(memory_space=pl.ANY)
PARAMS = pltpu.CompilerParams(vmem_limit_bytes=32 * 1024 * 1024)
PACK_PARAMS = pltpu.CompilerParams(vmem_limit_bytes=56 * 1024 * 1024)


def slot_of(chip, core):
    return chip ^ ((CHIPS - 1) * core)


def chip_at(slot, core):
    return slot ^ ((CHIPS - 1) * core)


def swap_sides(x):
    return pltpu.roll(x, SIDE, 1)


def left_side(rows):
    return lax.broadcasted_iota(jnp.int32, (rows, BLOCK), 1) < SIDE


def pack_kernel(ids, w_hbm, lw_hbm, ce_hbm, keep, send, drift, w, lw, ce, sems):
    core = ids[0]
    copies = [
        [
            pltpu.make_async_copy(src.at[mat], dst.at[mat], sems.at[kind, mat])
            for kind, (src, dst) in enumerate(((ce_hbm, ce), (w_hbm, w), (lw_hbm, lw)))
        ]
        for mat in range(MATS)
    ]
    for group in copies:
        for copy in group:
            copy.start()
    left = left_side(16)
    for block in range(BLOCKS, CHIPS):
        keep[slot_of(block, core)] = jnp.zeros((SHARE, BLOCK), jnp.float32)
        send[slot_of(block, 1 - core)] = jnp.zeros((SHARE, BLOCK), jnp.float32)
    for mat in range(MATS):
        for copy in copies[mat]:
            copy.wait()
        for block in range(BLOCKS):
            lanes = slice(block * BLOCK, (block + 1) * BLOCK)
            value = (
                w[mat, :, lanes].astype(jnp.float32)
                - lw[mat, :, lanes].astype(jnp.float32)
                + ce[mat, :, lanes]
            )
            drift[mat, :, lanes] = value
    for block in range(BLOCKS):
        lanes = slice(block * BLOCK, (block + 1) * BLOCK)
        keep[slot_of(block, core), 0:COLS] = drift[2 * core, :, lanes]
        send[slot_of(block, 1 - core), 0:COLS] = drift[2 - 2 * core, :, lanes]
        top, bottom = drift[1, 0:16, lanes], drift[1, 16:32, lanes]
        first = jnp.where(left, top, swap_sides(bottom))
        second = jnp.where(left, swap_sides(top), bottom)
        keep[slot_of(block, core), COLS:SHARE] = jnp.where(core == 0, first, second)
        send[slot_of(block, 1 - core), COLS:SHARE] = jnp.where(core == 0, second, first)


def outer(a, b):
    return lax.dot_general(
        a, b, (((1,), (1,)), ((), ())), precision=HIGHEST, preferred_element_type=jnp.float32
    )


def factor_kernel(ids, qt, got, inner, factor):
    core = ids[0]
    total = jnp.sum(got[...], axis=0)
    left = left_side(16)
    whole = total[0:COLS]
    half = total[COLS:SHARE]
    half = jnp.concatenate(
        [jnp.where(left, half, 0.0), jnp.where(left, swap_sides(half), 0.0)], axis=0
    )
    whole_factor = jnp.dot(
        qt[2 * core], whole, precision=HIGHEST, preferred_element_type=jnp.float32
    )
    half_factor = jnp.dot(qt[1], half, precision=HIGHEST, preferred_element_type=jnp.float32)
    factor[0:RANK] = whole_factor
    factor[RANK:FROWS] = half_factor[0:8] + swap_sides(half_factor[8:16])
    whole, half = outer(whole_factor, whole), outer(half_factor, half)
    inner[...] = jnp.concatenate([whole[0:8], whole[8:16], half[0:8], half[8:16]], axis=1)


def choose_kernel(ids, one, two, out):
    out[CHIPS * FROWS :] = jnp.sum(two[:, FROWS:GROWS], axis=0)
    for core, arrived in enumerate((one, two)):

        @pl.when(ids[0] == core)
        def _():
            for slot in range(CHIPS):
                out[slot * FROWS : slot * FROWS + FROWS] = arrived[slot, 0:FROWS]


def split(x):
    high = x.astype(jnp.bfloat16)
    rest = x - high.astype(jnp.float32)
    middle = rest.astype(jnp.bfloat16)
    return high, middle, (rest - middle.astype(jnp.float32)).astype(jnp.bfloat16)


def final_kernel(
    islands, ids, qt, own, sib, w, mom, drift,
    out_w, out_e, out_m, out_f, fac, buf_w, buf_e, buf_m, sems,
):
    first = ids[0] == 0

    rows = slice(CHIPS * FROWS, CHIPS * FROWS + MROWS)
    mine, other = own[rows], sib[rows]
    middle = pltpu.roll(mine + other, SIDE, 1)
    table = []
    for mat, rows in enumerate(
        (jnp.where(first, mine, other), middle, jnp.where(first, other, mine))
    ):
        rows = jnp.concatenate([rows[:, 0:COLS], rows[:, COLS : 2 * COLS]], axis=0)
        gram = outer(qt[mat], rows)
        rest = jnp.zeros((RANK, BLOCK - PAIR), jnp.float32)
        table.append(jnp.concatenate([gram, rows, rest], axis=1))
    table = jnp.stack(table)
    row = lax.broadcasted_iota(jnp.int32, table.shape, 1)
    small = table
    for step in range(0, RANK, 2):
        one = jnp.broadcast_to(table[:, :, step : step + 1], table.shape)
        two = jnp.broadcast_to(table[:, :, step + 1 : step + 2], table.shape)
        line = table[:, step : step + 1, :]
        pivot, cross = one[:, step : step + 1, :], two[:, step : step + 1, :]
        inverse = 1.0 / pivot
        ratio = one[:, step + 1 : step + 2, :] * inverse
        next_line = table[:, step + 1 : step + 2, :] - ratio * line
        next_pivot = two[:, step + 1 : step + 2, :] - ratio * cross
        next_scaled = next_line * (1.0 / next_pivot)
        scaled = (line - cross * next_scaled) * inverse
        here, below = row == step, row == step + 1
        small = jnp.where(here, line * lax.rsqrt(pivot), small)
        small = jnp.where(below, next_line * lax.rsqrt(next_pivot), small)
        rest = table - one * scaled - two * next_scaled
        table = jnp.where(here, scaled, jnp.where(below, next_scaled, rest))

    left = left_side(8)
    for block in range(BLOCKS):
        lanes = slice(block * BLOCK, (block + 1) * BLOCK)
        rows = slice(block * FROWS, block * FROWS + FROWS)
        mine, other = own[rows], sib[rows]
        low, high = jnp.where(first, mine, other), jnp.where(first, other, mine)
        low_half, high_half = low[RANK:FROWS], high[RANK:FROWS]
        half = jnp.concatenate(
            [
                jnp.where(left, low_half, swap_sides(high_half)),
                jnp.where(left, swap_sides(low_half), high_half),
            ],
            axis=0,
        )
        for mat, value in enumerate((low[0:RANK], half, high[0:RANK])):
            top, mid, last = split(value)
            for place, part in enumerate((top, mid, last, top, mid, top)):
                fac[mat, place * RANK : place * RANK + RANK, lanes] = part

    for mat in range(MATS):
        out_f[mat] = small[mat, :, RANK:PAIR] * (1.0 / islands)
        top, mid, last = split(table[mat, :, RANK:PAIR] * (1.0 / islands))
        parts = [x.astype(jnp.float32) for x in (top, top, top, mid, mid, last)]
        mixed = jnp.transpose(jnp.concatenate(parts, axis=0)).astype(jnp.bfloat16)
        for tile in range(7):
            lanes = slice(tile * 256, (tile + 1) * 256)
            approx = jnp.dot(mixed, fac[mat, :, lanes], preferred_element_type=jnp.float32)
            wide = w[mat, :, lanes].astype(jnp.float32)
            momentum = 0.9 * mom[mat, :, lanes] + approx
            buf_e[mat, :, lanes] = drift[mat, :, lanes] - approx
            buf_m[mat, :, lanes] = momentum
            buf_w[mat, :, lanes] = (wide - 0.7 * (approx + 0.9 * momentum)).astype(jnp.bfloat16)
        for kind, (buf, out) in enumerate(((buf_w, out_w), (buf_e, out_e), (buf_m, out_m))):
            pltpu.make_async_copy(buf.at[mat], out.at[mat], sems.at[kind, mat]).start()
    for mat in range(MATS):
        for kind, (buf, out) in enumerate(((buf_w, out_w), (buf_e, out_e), (buf_m, out_m))):
            pltpu.make_async_copy(buf.at[mat], out.at[mat], sems.at[kind, mat]).wait()


def sibling(x):
    return lax.ppermute(x, "replica", [(i, i ^ 1) for i in range(2 * CHIPS)])


def exchange_z(x):
    groups = [[2 * chip_at(slot, core) + core for slot in range(CHIPS)] for core in range(2)]
    return lax.all_to_all(x, "replica", 0, 0, axis_index_groups=groups, tiled=True)


def exchange_mixed(x, line_core):
    lines = [
        [(2 * chip + line_core) * 16 + place for chip in range(CHIPS)]
        for place in range(16)
    ]
    planes = [
        [(2 * chip + 1 - line_core) * 16 + place for place in range(16)] for chip in range(CHIPS)
    ]
    return lax.all_to_all(
        x, ("replica", "fsdp"), 0, 0, axis_index_groups=lines + planes, tiled=True
    )


def local(weights, local_weights, carried_error, momentum, initial_factor):
    f32 = jnp.float32
    ids = (lax.axis_index("replica") & 1).astype(jnp.int32).reshape(1)
    shape = (MATS, COLS, WIDTH)
    keep, send, drift = pl.pallas_call(
        pack_kernel,
        out_shape=[pltpu.VMEM((CHIPS, SHARE, BLOCK), f32)] * 2 + [pltpu.VMEM(shape, f32)],
        in_specs=[SMEM, HBM, HBM, HBM],
        out_specs=[VMEM] * 3,
        scratch_shapes=[
            pltpu.VMEM(shape, jnp.bfloat16),
            pltpu.VMEM(shape, jnp.bfloat16),
            pltpu.VMEM(shape, f32),
            pltpu.SemaphoreType.DMA((3, 3)),
        ],
        compiler_params=PACK_PARAMS,
        name="pack",
    )(ids, weights, local_weights[0], carried_error[0])
    qt = jnp.swapaxes(initial_factor, 1, 2)
    shares = exchange_z(keep + sibling(send))
    inner, factor = pl.pallas_call(
        factor_kernel,
        out_shape=[
            jax.ShapeDtypeStruct((MROWS, BLOCK), f32),
            jax.ShapeDtypeStruct((FROWS, BLOCK), f32),
        ],
        in_specs=[SMEM, VMEM, VMEM],
        out_specs=[VMEM, VMEM],
        compiler_params=PARAMS,
        name="factor",
    )(ids, qt, shares)

    arrivals = []
    for line_core in (0, 1):
        arrivals.append(
            exchange_mixed(
                jnp.broadcast_to(jnp.concatenate([factor, inner]), (CHIPS, GROWS, BLOCK)),
                line_core,
            )
        )
        inner = jnp.sum(arrivals[-1][:, FROWS:], axis=0)
    own = pl.pallas_call(
        choose_kernel,
        out_shape=pltpu.VMEM((CHIPS * FROWS + MROWS, BLOCK), f32),
        in_specs=[SMEM, VMEM, VMEM],
        out_specs=VMEM,
        compiler_params=PARAMS,
        name="choose",
    )(ids, *arrivals)
    sib = sibling(own)

    next_weights, next_error, next_momentum, following = pl.pallas_call(
        lambda *refs: final_kernel(lax.axis_size("replica"), *refs),
        out_shape=[
            jax.ShapeDtypeStruct(shape, jnp.bfloat16),
            jax.ShapeDtypeStruct(shape, f32),
            jax.ShapeDtypeStruct(shape, f32),
            jax.ShapeDtypeStruct((MATS, RANK, COLS), f32),
        ],
        in_specs=[SMEM] + [VMEM] * 6,
        out_specs=[HBM, HBM, HBM, VMEM],
        scratch_shapes=[
            pltpu.VMEM((MATS, 6 * RANK, WIDTH), jnp.bfloat16),
            pltpu.VMEM(shape, jnp.bfloat16),
            pltpu.VMEM(shape, f32),
            pltpu.VMEM(shape, f32),
            pltpu.SemaphoreType.DMA((3, 3)),
        ],
        compiler_params=PARAMS,
        name="final",
    )(ids, qt, own, sib, weights, momentum, drift)
    return (next_weights, next_error[None], next_momentum, jnp.swapaxes(following, 1, 2))


def solution(mesh):
    return jax.shard_map(
        local,
        mesh=mesh,
        in_specs=(
            P(None, None, "fsdp"),
            P("replica", None, None, "fsdp"),
            P("replica", None, None, "fsdp"),
            P(None, None, "fsdp"),
            P(),
        ),
        out_specs=(
            P(None, None, "fsdp"),
            P("replica", None, None, "fsdp"),
            P(None, None, "fsdp"),
            P(),
        ),
        check_vma=False,
    )
```

profile of v0, /device:TPU:1, one launch (start us, length us, event | category | flops | bytes accessed | tf_op | source)
XLA Modules:
  0.0 88.9 jit_solution(13724683815920971988)
XLA Ops:
  0.6 1.6 %pack.1 = (f32[16,48,128]{2,1,0:T(8,128)S(1)}, f32[16,48,128]{2,1,0:T(8,128)S(1)}, f32[3,32,1792]{2,1,0:T(8,128)S(1)}) custom-call(s32[1]{0:T(128)} %bitcast.ids.refs_0_, bf16[3,32,1792]{2,1,0:T(8,128)(2,1)} %refs_4_.1, bf16[3,32,1792]{2,1,0:T(8,128)(2,1)} %bitcast.9, f32[3,32,1792]{2,1,0:T(8,128)} %bitcast.8), custom_call_target="tpu_custom_call" | custom-call | tf_op jit(solution)/shard_map/pack/pallas_call | solution.py:227
  2.3 8.8 %collective-permute-start = (f32[16,48,128]{2,1,0:T(8,128)S(1)}, f32[16,48,128]{2,1,0:T(8,128)S(1)}, u32[]{:S(2)}, u32[]{:S(2)}) collective-permute-start(f32[16,48,128]{2,1,0:T(8,128)S(1)} %get-tuple-element.14), channel_id=1, source_target_pairs={{0,16},{16,0},{32,48},{48,32},{64,80},{80,64},{96,112},{112,96},{1... | collective-permute-start | bytes 1179656 | tf_op jit(solution)/shard_map/ppermute | solution.py:202
  11.1 1.3 %collective-permute-done = f32[16,48,128]{2,1,0:T(8,128)S(1)} collective-permute-done((f32[16,48,128]{2,1,0:T(8,128)S(1)}, f32[16,48,128]{2,1,0:T(8,128)S(1)}, u32[]{:S(2)}, u32[]{:S(2)}) %collective-permute-start) | collective-permute-done | bytes 393248 | tf_op jit(solution)/shard_map/ppermute | solution.py:202
  12.4 0.1 add.3
  12.5 0.0 copy-start.2
  12.5 31.8 %all_to_all.15.got = f32[16,48,128]{2,1,0:T(8,128)S(1)} all-to-all(f32[16,48,128]{2,1,0:T(8,128)S(1)} %add.3), channel_id=1, replica_groups={{0,32,64,96,128,160,192,224,256,288,320,352,384,416,448,480},{496,464,4..., dimensions={0} | all-to-all | bytes 786432 | tf_op jit(solution)/shard_map/all_to_all | solution.py:207
  44.2 0.0 copy-done.2
  44.2 0.4 factor.1
  44.7 0.1 broadcast_in_dim.9
  44.7 14.1 %all_to_all.16.one = f32[16,32,128]{2,1,0:T(8,128)S(1)} all-to-all(f32[16,32,128]{2,1,0:T(8,128)S(1)} %broadcast_in_dim.9), channel_id=1, replica_groups={{0,32,64,96,128,160,192,224,256,288,320,352,384,416,448,480},{1,33,65,9..., dimensions={0} | all-to-all | bytes 524288 | tf_op jit(solution)/shard_map/all_to_all | solution.py:218
  58.9 0.0 copy-start.1
  58.9 20.1 %all_to_all.17.two = f32[16,32,128]{2,1,0:T(8,128)S(1)} all-to-all(f32[16,32,128]{2,1,0:T(8,128)S(1)} %broadcast_in_dim.10), channel_id=1, replica_groups={{16,48,80,112,144,176,208,240,272,304,336,368,400,432,464,496},{17,49,8..., dimensions={0} | all-to-all | bytes 524288 | tf_op jit(solution)/shard_map/all_to_all | solution.py:218
  79.0 0.0 copy-start
  79.0 5.5 %collective-permute-start.1 = (f32[392,128]{1,0:T(8,128)S(1)}, f32[392,128]{1,0:T(8,128)S(1)}, u32[]{:S(2)}, u32[]{:S(2)}) collective-permute-start(f32[392,128]{1,0:T(8,128)S(1)} %choose.1.refs_2_), channel_id=1, source_target_pairs={{0,16},{16,0},{32,48},{48,32},{64,80},{80,64},{96,112},{112,96},{1... | collective-permute-start | bytes 602120 | tf_op jit(solution)/shard_map/ppermute | solution.py:202
  84.5 1.1 %collective-permute-done.1.refs_3_ = f32[392,128]{1,0:T(8,128)S(1)} collective-permute-done((f32[392,128]{1,0:T(8,128)S(1)}, f32[392,128]{1,0:T(8,128)S(1)}, u32[]{:S(2)}, u32[]{:S(2)}) %collective-permute-start.1) | collective-permute-done | bytes 200736 | tf_op jit(solution)/shard_map/ppermute | solution.py:202
  85.5 0.0 copy-done.1
  85.5 0.0 copy-done
  85.5 3.4 %final.1 = (bf16[3,32,1792]{2,1,0:T(8,128)(2,1)}, f32[3,32,1792]{2,1,0:T(8,128)}, f32[3,32,1792]{2,1,0:T(8,128)}, f32[3,16,32]{2,1,0:T(8,128)}) custom-call(s32[1]{0:T(128)} %bitcast.ids.refs_0_, f32[3,16,32]{2,1,0:T(8,128)S(1)} %bitcast.7, f32[392,128]{1,0:T(8,128)S(1)} %choose.1.refs_2_, f32[392,128]{1,0:T(8,128)S(1)} %collective-permute-done.1.refs_3_, ...), custom_call_target="tpu_custom_call" | custom-call | tf_op jit(solution)/shard_map/final/pallas_call | solution.py:274
  (5 shorter events, 0.1 us)
Async XLA Ops:
  2.3 10.1 %collective-permute-start = (f32[16,48,128]{2,1,0:T(8,128)S(1)}, f32[16,48,128]{2,1,0:T(8,128)S(1)}, u32[]{:S(2)}, u32[]{:S(2)}) collective-permute-start(f32[16,48,128]{2,1,0:T(8,128)S(1)} %get-tuple-element.14), channel_id=1, source_target_pairs={{0,16},{16,0},{32,48},{48,32},{64,80},{80,64},{96,112},{112,96},{1... | collective-permute-start | bytes 1179656 | tf_op jit(solution)/shard_map/ppermute | solution.py:202
  12.5 31.8 %copy-start.2 = (f32[3,32,16]{1,2,0:T(8,128)S(1)}, f32[3,32,16]{1,2,0:T(8,128)}, u32[]{:S(2)}) copy-start(f32[3,32,16]{1,2,0:T(8,128)} %param.9) | copy-start | bytes 18436
  58.9 26.7 %copy-start.1 = (f32[3,32,1792]{2,1,0:T(8,128)S(1)}, f32[3,32,1792]{2,1,0:T(8,128)}, u32[]{:S(2)}) copy-start(f32[3,32,1792]{2,1,0:T(8,128)} %refs_5_.1) | copy-start | bytes 2064388
  79.0 6.6 %copy-start = (bf16[3,32,1792]{2,1,0:T(8,128)(2,1)S(1)}, bf16[3,32,1792]{2,1,0:T(8,128)(2,1)}, u32[]{:S(2)}) copy-start(bf16[3,32,1792]{2,1,0:T(8,128)(2,1)} %refs_4_.1) | copy-start | bytes 1032196
  79.0 6.5 %collective-permute-start.1 = (f32[392,128]{1,0:T(8,128)S(1)}, f32[392,128]{1,0:T(8,128)S(1)}, u32[]{:S(2)}, u32[]{:S(2)}) collective-permute-start(f32[392,128]{1,0:T(8,128)S(1)} %choose.1.refs_2_), channel_id=1, source_target_pairs={{0,16},{16,0},{32,48},{48,32},{64,80},{80,64},{96,112},{112,96},{1... | collective-permute-start | bytes 602120 | tf_op jit(solution)/shard_map/ppermute | solution.py:202
where the time goes:
time: 89.3 us; the launch traced here: 88.9 us
  blocking collectives  65.9 us (74%)
  starting transfers between devices  14.2 us (16%)
  Pallas kernels  5.47 us (6%)
  waiting for transfers between devices  2.38 us (3%)
    all_to_all x2, blocking collectives, exchange_mixed(): lax.all_to_all(x, ('replica', 'fsdp'), 0, 0, axis_index_groups=lines + pl...  34.2 us
    all_to_all x1, blocking collectives, exchange_z(): lax.all_to_all(x, 'replica', 0, 0, axis_index_groups=groups, tiled=True)  31.8 us
    ppermute x2, starting transfers between devices, sibling(): return lax.ppermute(x, 'replica', [(i, i ^ 1) for i in range(2 * CHIPS)])  14.2 us
    pallas_call x1, Pallas kernels, local(): pl.pallas_call(lambda *refs: final_kernel(lax.axis_size('replica'), *refs...  3.37 us
    ppermute x2, waiting for transfers between devices, sibling(): return lax.ppermute(x, 'replica', [(i, i ^ 1) for i in range(2 * CHIPS)])  2.38 us
  transfers between devices with their start and end apart: 2, of which 2 were waited for; matrix products, arithmetic and copies ran while one was open for 0% of the time, Pallas kernels for 0%

commit v1 on v0

--- a/solution.py
+++ b/solution.py
@@ -27,11 +27,15 @@
 
 
 def slot_of(chip, core):
-    return chip ^ ((CHIPS - 1) * core)
+    return ((13 * (chip - 3)) & 15) ^ (8 * core)
 
 
 def chip_at(slot, core):
-    return slot ^ ((CHIPS - 1) * core)
+    return (3 + 8 * core + 5 * slot) % CHIPS
+
+
+def gather_slot(chip):
+    return (9 * chip) % CHIPS
 
 
 def swap_sides(x):
@@ -162,8 +166,8 @@
     left = left_side(8)
     for block in range(BLOCKS):
         lanes = slice(block * BLOCK, (block + 1) * BLOCK)
-        rows = slice(block * FROWS, block * FROWS + FROWS)
-        mine, other = own[rows], sib[rows]
+        start = gather_slot(block) * FROWS
+        mine, other = own[start : start + FROWS], sib[start : start + FROWS]
         low, high = jnp.where(first, mine, other), jnp.where(first, other, mine)
         low_half, high_half = low[RANK:FROWS], high[RANK:FROWS]
         half = jnp.concatenate(
@@ -209,7 +213,7 @@
 
 def exchange_mixed(x, line_core):
     lines = [
-        [(2 * chip + line_core) * 16 + place for chip in range(CHIPS)]
+        [(2 * gather_slot(slot) + line_core) * 16 + place for slot in range(CHIPS)]
         for place in range(16)
     ]
     planes = [

time: 89.3 us -> 89.3 us (level)
    all_to_all x1, blocking collectives: 31.8 us -> 27.9 us  [exchange_z(): lax.all_to_all(x, 'replica', 0, 0, axis_index_groups=groups, tiled=True)]
    all_to_all x2, blocking collectives: 34.2 us -> 37.6 us  [exchange_mixed(): lax.all_to_all(x, ('replica', 'fsdp'), 0, 0, axis_index_groups=lines + pl...]
where the time goes in v1:
time: 89.3 us; the launch traced here: 89 us
  blocking collectives  65.5 us (73%)
  starting transfers between devices  14.8 us (17%)
  Pallas kernels  5.47 us (6%)
  waiting for transfers between devices  2.38 us (3%)
    all_to_all x2, blocking collectives, exchange_mixed(): lax.all_to_all(x, ('replica', 'fsdp'), 0, 0, axis_index_groups=lines + pl...  37.6 us
    all_to_all x1, blocking collectives, exchange_z(): lax.all_to_all(x, 'replica', 0, 0, axis_index_groups=groups, tiled=True)  27.9 us
    ppermute x2, starting transfers between devices, sibling(): return lax.ppermute(x, 'replica', [(i, i ^ 1) for i in range(2 * CHIPS)])  14.8 us
    pallas_call x1, Pallas kernels, local(): pl.pallas_call(lambda *refs: final_kernel(lax.axis_size('replica'), *refs...  3.37 us
    ppermute x2, waiting for transfers between devices, sibling(): return lax.ppermute(x, 'replica', [(i, i ^ 1) for i in range(2 * CHIPS)])  2.38 us
  transfers between devices with their start and end apart: 2, of which 2 were waited for; matrix products, arithmetic and copies ran while one was open for 0% of the time, Pallas kernels for 0%

profile of v1, /device:TPU:1, one launch (start us, length us, event | category | flops | bytes accessed | tf_op | source)
XLA Modules:
  0.0 89.0 jit_solution(11232909773711314308)
XLA Ops:
  0.6 1.6 %pack.1 = (f32[16,48,128]{2,1,0:T(8,128)S(1)}, f32[16,48,128]{2,1,0:T(8,128)S(1)}, f32[3,32,1792]{2,1,0:T(8,128)S(1)}) custom-call(s32[1]{0:T(128)} %bitcast.ids.refs_0_, bf16[3,32,1792]{2,1,0:T(8,128)(2,1)} %refs_4_.1, bf16[3,32,1792]{2,1,0:T(8,128)(2,1)} %bitcast.9, f32[3,32,1792]{2,1,0:T(8,128)} %bitcast.8), custom_call_target="tpu_custom_call" | custom-call | tf_op jit(solution)/shard_map/pack/pallas_call | solution.py:231
  2.3 8.8 %collective-permute-start = (f32[16,48,128]{2,1,0:T(8,128)S(1)}, f32[16,48,128]{2,1,0:T(8,128)S(1)}, u32[]{:S(2)}, u32[]{:S(2)}) collective-permute-start(f32[16,48,128]{2,1,0:T(8,128)S(1)} %get-tuple-element.14), channel_id=1, source_target_pairs={{0,16},{16,0},{32,48},{48,32},{64,80},{80,64},{96,112},{112,96},{1... | collective-permute-start | bytes 1179656 | tf_op jit(solution)/shard_map/ppermute | solution.py:206
  11.1 1.3 %collective-permute-done = f32[16,48,128]{2,1,0:T(8,128)S(1)} collective-permute-done((f32[16,48,128]{2,1,0:T(8,128)S(1)}, f32[16,48,128]{2,1,0:T(8,128)S(1)}, u32[]{:S(2)}, u32[]{:S(2)}) %collective-permute-start) | collective-permute-done | bytes 393248 | tf_op jit(solution)/shard_map/ppermute | solution.py:206
  12.4 0.1 add.3
  12.5 0.0 copy-start.2
  12.5 27.9 %all_to_all.15.got = f32[16,48,128]{2,1,0:T(8,128)S(1)} all-to-all(f32[16,48,128]{2,1,0:T(8,128)S(1)} %add.3), channel_id=1, replica_groups={{96,256,416,64,224,384,32,192,352,0,160,320,480,128,288,448},{368,16,17..., dimensions={0} | all-to-all | bytes 786432 | tf_op jit(solution)/shard_map/all_to_all | solution.py:211
  40.3 0.0 copy-done.2
  40.3 0.4 factor.1
  40.8 0.1 broadcast_in_dim.9
  40.8 14.1 %all_to_all.16.one = f32[16,32,128]{2,1,0:T(8,128)S(1)} all-to-all(f32[16,32,128]{2,1,0:T(8,128)S(1)} %broadcast_in_dim.9), channel_id=1, replica_groups={{0,288,64,352,128,416,192,480,256,32,320,96,384,160,448,224},{1,289,65,..., dimensions={0} | all-to-all | bytes 524288 | tf_op jit(solution)/shard_map/all_to_all | solution.py:222
  55.0 0.0 copy-start.1
  55.0 23.5 %all_to_all.17.two = f32[16,32,128]{2,1,0:T(8,128)S(1)} all-to-all(f32[16,32,128]{2,1,0:T(8,128)S(1)} %broadcast_in_dim.10), channel_id=1, replica_groups={{16,304,80,368,144,432,208,496,272,48,336,112,400,176,464,240},{17,305,..., dimensions={0} | all-to-all | bytes 524288 | tf_op jit(solution)/shard_map/all_to_all | solution.py:222
  78.5 0.0 copy-start
  78.6 6.0 %collective-permute-start.1 = (f32[392,128]{1,0:T(8,128)S(1)}, f32[392,128]{1,0:T(8,128)S(1)}, u32[]{:S(2)}, u32[]{:S(2)}) collective-permute-start(f32[392,128]{1,0:T(8,128)S(1)} %choose.1.refs_2_), channel_id=1, source_target_pairs={{0,16},{16,0},{32,48},{48,32},{64,80},{80,64},{96,112},{112,96},{1... | collective-permute-start | bytes 602120 | tf_op jit(solution)/shard_map/ppermute | solution.py:206
  84.5 1.1 %collective-permute-done.1.refs_3_ = f32[392,128]{1,0:T(8,128)S(1)} collective-permute-done((f32[392,128]{1,0:T(8,128)S(1)}, f32[392,128]{1,0:T(8,128)S(1)}, u32[]{:S(2)}, u32[]{:S(2)}) %collective-permute-start.1) | collective-permute-done | bytes 200736 | tf_op jit(solution)/shard_map/ppermute | solution.py:206
  85.6 0.0 copy-done.1
  85.6 0.0 copy-done
  85.6 3.4 %final.1 = (bf16[3,32,1792]{2,1,0:T(8,128)(2,1)}, f32[3,32,1792]{2,1,0:T(8,128)}, f32[3,32,1792]{2,1,0:T(8,128)}, f32[3,16,32]{2,1,0:T(8,128)}) custom-call(s32[1]{0:T(128)} %bitcast.ids.refs_0_, f32[3,16,32]{2,1,0:T(8,128)S(1)} %bitcast.7, f32[392,128]{1,0:T(8,128)S(1)} %choose.1.refs_2_, f32[392,128]{1,0:T(8,128)S(1)} %collective-permute-done.1.refs_3_, ...), custom_call_target="tpu_custom_call" | custom-call | tf_op jit(solution)/shard_map/final/pallas_call | solution.py:278
  (5 shorter events, 0.1 us)
Async XLA Ops:
  2.3 10.1 %collective-permute-start = (f32[16,48,128]{2,1,0:T(8,128)S(1)}, f32[16,48,128]{2,1,0:T(8,128)S(1)}, u32[]{:S(2)}, u32[]{:S(2)}) collective-permute-start(f32[16,48,128]{2,1,0:T(8,128)S(1)} %get-tuple-element.14), channel_id=1, source_target_pairs={{0,16},{16,0},{32,48},{48,32},{64,80},{80,64},{96,112},{112,96},{1... | collective-permute-start | bytes 1179656 | tf_op jit(solution)/shard_map/ppermute | solution.py:206
  12.5 27.9 %copy-start.2 = (f32[3,32,16]{1,2,0:T(8,128)S(1)}, f32[3,32,16]{1,2,0:T(8,128)}, u32[]{:S(2)}) copy-start(f32[3,32,16]{1,2,0:T(8,128)} %param.9) | copy-start | bytes 18436
  55.0 30.6 %copy-start.1 = (f32[3,32,1792]{2,1,0:T(8,128)S(1)}, f32[3,32,1792]{2,1,0:T(8,128)}, u32[]{:S(2)}) copy-start(f32[3,32,1792]{2,1,0:T(8,128)} %refs_5_.1) | copy-start | bytes 2064388
  78.5 7.1 %copy-start = (bf16[3,32,1792]{2,1,0:T(8,128)(2,1)S(1)}, bf16[3,32,1792]{2,1,0:T(8,128)(2,1)}, u32[]{:S(2)}) copy-start(bf16[3,32,1792]{2,1,0:T(8,128)(2,1)} %refs_4_.1) | copy-start | bytes 1032196
  78.6 7.0 %collective-permute-start.1 = (f32[392,128]{1,0:T(8,128)S(1)}, f32[392,128]{1,0:T(8,128)S(1)}, u32[]{:S(2)}, u32[]{:S(2)}) collective-permute-start(f32[392,128]{1,0:T(8,128)S(1)} %choose.1.refs_2_), channel_id=1, source_target_pairs={{0,16},{16,0},{32,48},{48,32},{64,80},{80,64},{96,112},{112,96},{1... | collective-permute-start | bytes 602120 | tf_op jit(solution)/shard_map/ppermute | solution.py:206

commit v2 on v1

--- a/solution.py
+++ b/solution.py
@@ -111,7 +111,7 @@
 
 def choose_kernel(ids, one, two, out):
     out[CHIPS * FROWS :] = jnp.sum(two[:, FROWS:GROWS], axis=0)
-    for core, arrived in enumerate((one, two)):
+    for core, arrived in enumerate((two, one)):
 
         @pl.when(ids[0] == core)
         def _():
@@ -257,7 +257,7 @@
     )(ids, qt, shares)
 
     arrivals = []
-    for line_core in (0, 1):
+    for line_core in (1, 0):
         arrivals.append(
             exchange_mixed(
                 jnp.broadcast_to(jnp.concatenate([factor, inner]), (CHIPS, GROWS, BLOCK)),

time: 89.3 us -> 89.3 us (level)
  no operation moved by 1% of the time
where the time goes in v2:
time: 89.3 us; the launch traced here: 89 us
  blocking collectives  65.5 us (73%)
  starting transfers between devices  14.7 us (16%)
  Pallas kernels  5.47 us (6%)
  waiting for transfers between devices  2.38 us (3%)
    all_to_all x2, blocking collectives, exchange_mixed(): lax.all_to_all(x, ('replica', 'fsdp'), 0, 0, axis_index_groups=lines + pl...  37.6 us
    all_to_all x1, blocking collectives, exchange_z(): lax.all_to_all(x, 'replica', 0, 0, axis_index_groups=groups, tiled=True)  27.9 us
    ppermute x2, starting transfers between devices, sibling(): return lax.ppermute(x, 'replica', [(i, i ^ 1) for i in range(2 * CHIPS)])  14.7 us
    pallas_call x1, Pallas kernels, local(): pl.pallas_call(lambda *refs: final_kernel(lax.axis_size('replica'), *refs...  3.37 us
    ppermute x2, waiting for transfers between devices, sibling(): return lax.ppermute(x, 'replica', [(i, i ^ 1) for i in range(2 * CHIPS)])  2.38 us
  transfers between devices with their start and end apart: 2, of which 2 were waited for; matrix products, arithmetic and copies ran while one was open for 0% of the time, Pallas kernels for 0%

profile of v2, /device:TPU:1, one launch (start us, length us, event | category | flops | bytes accessed | tf_op | source)
XLA Modules:
  0.0 89.0 jit_solution(16895693110410740393)
XLA Ops:
  0.6 1.6 %pack.1 = (f32[16,48,128]{2,1,0:T(8,128)S(1)}, f32[16,48,128]{2,1,0:T(8,128)S(1)}, f32[3,32,1792]{2,1,0:T(8,128)S(1)}) custom-call(s32[1]{0:T(128)} %bitcast.ids.refs_0_, bf16[3,32,1792]{2,1,0:T(8,128)(2,1)} %refs_4_.1, bf16[3,32,1792]{2,1,0:T(8,128)(2,1)} %bitcast.9, f32[3,32,1792]{2,1,0:T(8,128)} %bitcast.8), custom_call_target="tpu_custom_call" | custom-call | tf_op jit(solution)/shard_map/pack/pallas_call | solution.py:231
  2.3 8.8 %collective-permute-start = (f32[16,48,128]{2,1,0:T(8,128)S(1)}, f32[16,48,128]{2,1,0:T(8,128)S(1)}, u32[]{:S(2)}, u32[]{:S(2)}) collective-permute-start(f32[16,48,128]{2,1,0:T(8,128)S(1)} %get-tuple-element.14), channel_id=1, source_target_pairs={{0,16},{16,0},{32,48},{48,32},{64,80},{80,64},{96,112},{112,96},{1... | collective-permute-start | bytes 1179656 | tf_op jit(solution)/shard_map/ppermute | solution.py:206
  11.1 1.3 %collective-permute-done = f32[16,48,128]{2,1,0:T(8,128)S(1)} collective-permute-done((f32[16,48,128]{2,1,0:T(8,128)S(1)}, f32[16,48,128]{2,1,0:T(8,128)S(1)}, u32[]{:S(2)}, u32[]{:S(2)}) %collective-permute-start) | collective-permute-done | bytes 393248 | tf_op jit(solution)/shard_map/ppermute | solution.py:206
  12.4 0.1 add.3
  12.5 0.0 copy-start.2
  12.5 27.9 %all_to_all.15.got = f32[16,48,128]{2,1,0:T(8,128)S(1)} all-to-all(f32[16,48,128]{2,1,0:T(8,128)S(1)} %add.3), channel_id=1, replica_groups={{96,256,416,64,224,384,32,192,352,0,160,320,480,128,288,448},{368,16,17..., dimensions={0} | all-to-all | bytes 786432 | tf_op jit(solution)/shard_map/all_to_all | solution.py:211
  40.3 0.0 copy-done.2
  40.3 0.4 factor.1
  40.8 0.1 broadcast_in_dim.9
  40.8 23.1 %all_to_all.16.one = f32[16,32,128]{2,1,0:T(8,128)S(1)} all-to-all(f32[16,32,128]{2,1,0:T(8,128)S(1)} %broadcast_in_dim.9), channel_id=1, replica_groups={{16,304,80,368,144,432,208,496,272,48,336,112,400,176,464,240},{17,305,..., dimensions={0} | all-to-all | bytes 524288 | tf_op jit(solution)/shard_map/all_to_all | solution.py:222
  64.0 0.0 copy-start.1
  64.0 14.5 %all_to_all.17.two = f32[16,32,128]{2,1,0:T(8,128)S(1)} all-to-all(f32[16,32,128]{2,1,0:T(8,128)S(1)} %broadcast_in_dim.10), channel_id=1, replica_groups={{0,288,64,352,128,416,192,480,256,32,320,96,384,160,448,224},{1,289,65,..., dimensions={0} | all-to-all | bytes 524288 | tf_op jit(solution)/shard_map/all_to_all | solution.py:222
  78.5 0.0 copy-start
  78.6 6.0 %collective-permute-start.1 = (f32[392,128]{1,0:T(8,128)S(1)}, f32[392,128]{1,0:T(8,128)S(1)}, u32[]{:S(2)}, u32[]{:S(2)}) collective-permute-start(f32[392,128]{1,0:T(8,128)S(1)} %choose.1.refs_2_), channel_id=1, source_target_pairs={{0,16},{16,0},{32,48},{48,32},{64,80},{80,64},{96,112},{112,96},{1... | collective-permute-start | bytes 602120 | tf_op jit(solution)/shard_map/ppermute | solution.py:206
  84.5 1.1 %collective-permute-done.1.refs_3_ = f32[392,128]{1,0:T(8,128)S(1)} collective-permute-done((f32[392,128]{1,0:T(8,128)S(1)}, f32[392,128]{1,0:T(8,128)S(1)}, u32[]{:S(2)}, u32[]{:S(2)}) %collective-permute-start.1) | collective-permute-done | bytes 200736 | tf_op jit(solution)/shard_map/ppermute | solution.py:206
  85.6 0.0 copy-done.1
  85.6 0.0 copy-done
  85.6 3.4 %final.1 = (bf16[3,32,1792]{2,1,0:T(8,128)(2,1)}, f32[3,32,1792]{2,1,0:T(8,128)}, f32[3,32,1792]{2,1,0:T(8,128)}, f32[3,16,32]{2,1,0:T(8,128)}) custom-call(s32[1]{0:T(128)} %bitcast.ids.refs_0_, f32[3,16,32]{2,1,0:T(8,128)S(1)} %bitcast.7, f32[392,128]{1,0:T(8,128)S(1)} %choose.1.refs_2_, f32[392,128]{1,0:T(8,128)S(1)} %collective-permute-done.1.refs_3_, ...), custom_call_target="tpu_custom_call" | custom-call | tf_op jit(solution)/shard_map/final/pallas_call | solution.py:278
  (5 shorter events, 0.1 us)
Async XLA Ops:
  2.3 10.1 %collective-permute-start = (f32[16,48,128]{2,1,0:T(8,128)S(1)}, f32[16,48,128]{2,1,0:T(8,128)S(1)}, u32[]{:S(2)}, u32[]{:S(2)}) collective-permute-start(f32[16,48,128]{2,1,0:T(8,128)S(1)} %get-tuple-element.14), channel_id=1, source_target_pairs={{0,16},{16,0},{32,48},{48,32},{64,80},{80,64},{96,112},{112,96},{1... | collective-permute-start | bytes 1179656 | tf_op jit(solution)/shard_map/ppermute | solution.py:206
  12.5 27.9 %copy-start.2 = (f32[3,32,16]{1,2,0:T(8,128)S(1)}, f32[3,32,16]{1,2,0:T(8,128)}, u32[]{:S(2)}) copy-start(f32[3,32,16]{1,2,0:T(8,128)} %param.9) | copy-start | bytes 18436
  64.0 21.6 %copy-start.1 = (f32[3,32,1792]{2,1,0:T(8,128)S(1)}, f32[3,32,1792]{2,1,0:T(8,128)}, u32[]{:S(2)}) copy-start(f32[3,32,1792]{2,1,0:T(8,128)} %refs_5_.1) | copy-start | bytes 2064388
  78.5 7.1 %copy-start = (bf16[3,32,1792]{2,1,0:T(8,128)(2,1)S(1)}, bf16[3,32,1792]{2,1,0:T(8,128)(2,1)}, u32[]{:S(2)}) copy-start(bf16[3,32,1792]{2,1,0:T(8,128)(2,1)} %refs_4_.1) | copy-start | bytes 1032196
  78.6 7.0 %collective-permute-start.1 = (f32[392,128]{1,0:T(8,128)S(1)}, f32[392,128]{1,0:T(8,128)S(1)}, u32[]{:S(2)}, u32[]{:S(2)}) collective-permute-start(f32[392,128]{1,0:T(8,128)S(1)} %choose.1.refs_2_), channel_id=1, source_target_pairs={{0,16},{16,0},{32,48},{48,32},{64,80},{80,64},{96,112},{112,96},{1... | collective-permute-start | bytes 602120 | tf_op jit(solution)/shard_map/ppermute | solution.py:206

commit v3 on v1

--- a/solution.py
+++ b/solution.py
@@ -46,7 +46,47 @@
     return lax.broadcasted_iota(jnp.int32, (rows, BLOCK), 1) < SIDE
 
 
-def pack_kernel(ids, w_hbm, lw_hbm, ce_hbm, keep, send, drift, w, lw, ce, sems):
+def corrected(w, lw, ce, mat, lanes):
+    return (
+        w[mat, :, lanes].astype(jnp.float32)
+        - lw[mat, :, lanes].astype(jnp.float32)
+        + ce[mat, :, lanes]
+    )
+
+
+def half_block(value, core):
+    left = left_side(16)
+    top, bottom = value[0:16], value[16:32]
+    first = jnp.where(left, top, swap_sides(bottom))
+    second = jnp.where(left, swap_sides(top), bottom)
+    return jnp.where(core == 0, first, second)
+
+
+def send_kernel(ids, w_hbm, lw_hbm, ce_hbm, send, ids_out, w, lw, ce, sems):
+    other = 1 - ids[0]
+    ids_out[0] = ids[0]
+    copies = [
+        [
+            pltpu.make_async_copy(src.at[mat], dst.at[place], sems.at[kind, place])
+            for kind, (src, dst) in enumerate(((ce_hbm, ce), (w_hbm, w), (lw_hbm, lw)))
+        ]
+        for place, mat in enumerate((1, 2 * other))
+    ]
+    for group in copies:
+        for copy in group:
+            copy.start()
+    for block in range(BLOCKS, CHIPS):
+        send[slot_of(block, other)] = jnp.zeros((SHARE, BLOCK), jnp.float32)
+    for place, rows in enumerate((slice(COLS, SHARE), slice(0, COLS))):
+        for copy in copies[place]:
+            copy.wait()
+        for block in range(BLOCKS):
+            lanes = slice(block * BLOCK, (block + 1) * BLOCK)
+            value = corrected(w, lw, ce, place, lanes)
+            send[slot_of(block, other), rows] = half_block(value, other) if place == 0 else value
+
+
+def keep_kernel(ids, w_hbm, lw_hbm, ce_hbm, keep, drift, w, lw, ce, sems):
     core = ids[0]
     copies = [
         [
@@ -58,30 +98,18 @@
     for group in copies:
         for copy in group:
             copy.start()
-    left = left_side(16)
     for block in range(BLOCKS, CHIPS):
         keep[slot_of(block, core)] = jnp.zeros((SHARE, BLOCK), jnp.float32)
-        send[slot_of(block, 1 - core)] = jnp.zeros((SHARE, BLOCK), jnp.float32)
     for mat in range(MATS):
         for copy in copies[mat]:
             copy.wait()
         for block in range(BLOCKS):
             lanes = slice(block * BLOCK, (block + 1) * BLOCK)
-            value = (
-                w[mat, :, lanes].astype(jnp.float32)
-                - lw[mat, :, lanes].astype(jnp.float32)
-                + ce[mat, :, lanes]
-            )
-            drift[mat, :, lanes] = value
+            drift[mat, :, lanes] = corrected(w, lw, ce, mat, lanes)
     for block in range(BLOCKS):
         lanes = slice(block * BLOCK, (block + 1) * BLOCK)
         keep[slot_of(block, core), 0:COLS] = drift[2 * core, :, lanes]
-        send[slot_of(block, 1 - core), 0:COLS] = drift[2 - 2 * core, :, lanes]
-        top, bottom = drift[1, 0:16, lanes], drift[1, 16:32, lanes]
-        first = jnp.where(left, top, swap_sides(bottom))
-        second = jnp.where(left, swap_sides(top), bottom)
-        keep[slot_of(block, core), COLS:SHARE] = jnp.where(core == 0, first, second)
-        send[slot_of(block, 1 - core), COLS:SHARE] = jnp.where(core == 0, second, first)
+        keep[slot_of(block, core), COLS:SHARE] = half_block(drift[1, :, lanes], core)
 
 
 def outer(a, b):
@@ -109,6 +137,14 @@
     inner[...] = jnp.concatenate([whole[0:8], whole[8:16], half[0:8], half[8:16]], axis=1)
 
 
+def stacked(a, b):
+    a_top, a_mid, a_last = split(a)
+    b_top, b_mid, b_last = split(b)
+    a = jnp.concatenate([a_top, a_top, a_top, a_mid, a_mid, a_last], axis=1)
+    b = jnp.concatenate([b_top, b_mid, b_last, b_top, b_mid, b_top], axis=1)
+    return lax.dot_general(a, b, (((1,), (1,)), ((), ())), preferred_element_type=jnp.float32)
+
+
 def choose_kernel(ids, one, two, out):
     out[CHIPS * FROWS :] = jnp.sum(two[:, FROWS:GROWS], axis=0)
     for core, arrived in enumerate((one, two)):
@@ -140,7 +176,7 @@
         (jnp.where(first, mine, other), middle, jnp.where(first, other, mine))
     ):
         rows = jnp.concatenate([rows[:, 0:COLS], rows[:, COLS : 2 * COLS]], axis=0)
-        gram = outer(qt[mat], rows)
+        gram = stacked(qt[mat], rows)
         rest = jnp.zeros((RANK, BLOCK - PAIR), jnp.float32)
         table.append(jnp.concatenate([gram, rows, rest], axis=1))
     table = jnp.stack(table)
@@ -228,11 +264,27 @@
     f32 = jnp.float32
     ids = (lax.axis_index("replica") & 1).astype(jnp.int32).reshape(1)
     shape = (MATS, COLS, WIDTH)
-    keep, send, drift = pl.pallas_call(
-        pack_kernel,
-        out_shape=[pltpu.VMEM((CHIPS, SHARE, BLOCK), f32)] * 2 + [pltpu.VMEM(shape, f32)],
+    arrays = (weights, local_weights[0], carried_error[0])
+    send, ids_after = pl.pallas_call(
+        send_kernel,
+        out_shape=[pltpu.VMEM((CHIPS, SHARE, BLOCK), f32), pltpu.SMEM((1,), jnp.int32)],
         in_specs=[SMEM, HBM, HBM, HBM],
-        out_specs=[VMEM] * 3,
+        out_specs=[VMEM, SMEM],
+        scratch_shapes=[
+            pltpu.VMEM((2, COLS, WIDTH), jnp.bfloat16),
+            pltpu.VMEM((2, COLS, WIDTH), jnp.bfloat16),
+            pltpu.VMEM((2, COLS, WIDTH), f32),
+            pltpu.SemaphoreType.DMA((3, 2)),
+        ],
+        compiler_params=PACK_PARAMS,
+        name="pack_send",
+    )(ids, *arrays)
+    got = sibling(send)
+    keep, drift = pl.pallas_call(
+        keep_kernel,
+        out_shape=[pltpu.VMEM((CHIPS, SHARE, BLOCK), f32), pltpu.VMEM(shape, f32)],
+        in_specs=[SMEM, HBM, HBM, HBM],
+        out_specs=[VMEM] * 2,
         scratch_shapes=[
             pltpu.VMEM(shape, jnp.bfloat16),
             pltpu.VMEM(shape, jnp.bfloat16),
@@ -240,10 +292,13 @@
             pltpu.SemaphoreType.DMA((3, 3)),
         ],
         compiler_params=PACK_PARAMS,
-        name="pack",
-    )(ids, weights, local_weights[0], carried_error[0])
+        cost_estimate=pl.CostEstimate(
+            flops=1_000_000, bytes_accessed=4_000_000, transcendentals=0
+        ),
+        name="pack_keep",
+    )(ids_after, *arrays)
     qt = jnp.swapaxes(initial_factor, 1, 2)
-    shares = exchange_z(keep + sibling(send))
+    shares = exchange_z(keep + got)
     inner, factor = pl.pallas_call(
         factor_kernel,
         out_shape=[

time: 89.3 us -> 88.8 us (level)
  Pallas kernels: 5.47 us -> 6.88 us
  waiting for transfers between devices: 2.38 us -> 1.06 us
    pallas_call x1 -> x2, Pallas kernels: 1.64 us -> 3 us  [the longest x1 1.64 us: local(): pl.pallas_call(keep_kernel, out_shape=[pltpu.VMEM((CHIPS, SHARE, BLOCK),...]
    ppermute x2, waiting for transfers between devices: 2.38 us -> 1.06 us  [sibling(): return lax.ppermute(x, 'replica', [(i, i ^ 1) for i in range(2 * CHIPS)])]
  transfers between devices with their start and end apart: 2 -> 2, of which waited for: 2 -> 1; matrix products, arithmetic and copies ran while one was open for 0% -> 0% of each run, Pallas kernels for 0% -> 2%
where the time goes in v3:
time: 88.8 us; the launch traced here: 88.4 us
  blocking collectives  65.3 us (74%)
  starting transfers between devices  14.2 us (16%)
  Pallas kernels  6.88 us (8%)
  waiting for transfers between devices  1.06 us (1%)
    all_to_all x2, blocking collectives, exchange_mixed(): lax.all_to_all(x, ('replica', 'fsdp'), 0, 0, axis_index_groups=lines + pl...  38 us
    all_to_all x1, blocking collectives, exchange_z(): lax.all_to_all(x, 'replica', 0, 0, axis_index_groups=groups, tiled=True)  27.3 us
    ppermute x2, starting transfers between devices, sibling(): return lax.ppermute(x, 'replica', [(i, i ^ 1) for i in range(2 * CHIPS)])  14.2 us
    pallas_call x1, Pallas kernels, local(): pl.pallas_call(lambda *refs: final_kernel(lax.axis_size('replica'), *refs...  3.42 us
  transfers between devices with their start and end apart: 2, of which 1 were waited for; matrix products, arithmetic and copies ran while one was open for 0% of the time, Pallas kernels for 2%

profile of v3, /device:TPU:1, one launch (start us, length us, event | category | flops | bytes accessed | tf_op | source)
XLA Modules:
  0.0 88.4 jit_solution(2957064401179302601)
XLA Ops:
  0.6 1.4 %pack_send.1 = (f32[16,48,128]{2,1,0:T(8,128)S(1)}, s32[1]{0:T(128)S(4)}) custom-call(s32[1]{0:T(128)} %bitcast.ids.refs_0_, bf16[3,32,1792]{2,1,0:T(8,128)(2,1)} %refs_4_.1, bf16[3,32,1792]{2,1,0:T(8,128)(2,1)} %bitcast.10, f32[3,32,1792]{2,1,0:T(8,128)} %bitcast.8), custom_call_target="tpu_custom_call" | custom-call | tf_op jit(solution)/shard_map/pack_send/pallas_call | solution.py:268
  2.0 8.8 %collective-permute-start = (f32[16,48,128]{2,1,0:T(8,128)S(1)}, f32[16,48,128]{2,1,0:T(8,128)S(1)}, u32[]{:S(2)}, u32[]{:S(2)}) collective-permute-start(f32[16,48,128]{2,1,0:T(8,128)S(1)} %get-tuple-element.16), channel_id=1, source_target_pairs={{0,16},{16,0},{32,48},{48,32},{64,80},{80,64},{96,112},{112,96},{1... | collective-permute-start | bytes 1179656 | tf_op jit(solution)/shard_map/ppermute | solution.py:242
  10.8 1.6 %pack_keep.1 = (f32[16,48,128]{2,1,0:T(8,128)S(1)}, f32[3,32,1792]{2,1,0:T(8,128)S(1)}) custom-call(s32[1]{0:T(128)S(4)} %get-tuple-element.14.ids, bf16[3,32,1792]{2,1,0:T(8,128)(2,1)} %refs_4_.1, bf16[3,32,1792]{2,1,0:T(8,128)(2,1)} %bitcast.11, f32[3,32,1792]{2,1,0:T(8,128)} %bitcast.9), custom_call_target="tpu_custom_call" | custom-call | flops 1000000 | bytes 4000000 | tf_op jit(solution)/shard_map/pack_keep/pallas_call | solution.py:283
  12.4 0.0 collective-permute-done
  12.5 0.0 copy-start.2
  12.5 27.3 %all_to_all.15.got = f32[16,48,128]{2,1,0:T(8,128)S(1)} all-to-all(f32[16,48,128]{2,1,0:T(8,128)S(1)} %add.3), channel_id=1, replica_groups={{96,256,416,64,224,384,32,192,352,0,160,320,480,128,288,448},{368,16,17..., dimensions={0} | all-to-all | bytes 786432 | tf_op jit(solution)/shard_map/all_to_all | solution.py:247
  39.8 0.0 copy-done.2
  39.8 0.4 factor.1
  40.3 0.1 broadcast_in_dim.9
  40.3 14.1 %all_to_all.16.one = f32[16,32,128]{2,1,0:T(8,128)S(1)} all-to-all(f32[16,32,128]{2,1,0:T(8,128)S(1)} %broadcast_in_dim.9), channel_id=1, replica_groups={{0,288,64,352,128,416,192,480,256,32,320,96,384,160,448,224},{1,289,65,..., dimensions={0} | all-to-all | bytes 524288 | tf_op jit(solution)/shard_map/all_to_all | solution.py:258
  54.5 0.0 copy-start.1
  54.5 23.9 %all_to_all.17.two = f32[16,32,128]{2,1,0:T(8,128)S(1)} all-to-all(f32[16,32,128]{2,1,0:T(8,128)S(1)} %broadcast_in_dim.10), channel_id=1, replica_groups={{16,304,80,368,144,432,208,496,272,48,336,112,400,176,464,240},{17,305,..., dimensions={0} | all-to-all | bytes 524288 | tf_op jit(solution)/shard_map/all_to_all | solution.py:258
  78.4 0.0 copy-start
  78.5 5.4 %collective-permute-start.1 = (f32[392,128]{1,0:T(8,128)S(1)}, f32[392,128]{1,0:T(8,128)S(1)}, u32[]{:S(2)}, u32[]{:S(2)}) collective-permute-start(f32[392,128]{1,0:T(8,128)S(1)} %choose.1.refs_2_), channel_id=1, source_target_pairs={{0,16},{16,0},{32,48},{48,32},{64,80},{80,64},{96,112},{112,96},{1... | collective-permute-start | bytes 602120 | tf_op jit(solution)/shard_map/ppermute | solution.py:242
  83.9 1.1 %collective-permute-done.1.refs_3_ = f32[392,128]{1,0:T(8,128)S(1)} collective-permute-done((f32[392,128]{1,0:T(8,128)S(1)}, f32[392,128]{1,0:T(8,128)S(1)}, u32[]{:S(2)}, u32[]{:S(2)}) %collective-permute-start.1) | collective-permute-done | bytes 200736 | tf_op jit(solution)/shard_map/ppermute | solution.py:242
  85.0 0.0 copy-done.1
  85.0 0.0 copy-done
  85.0 3.4 %final.1 = (bf16[3,32,1792]{2,1,0:T(8,128)(2,1)}, f32[3,32,1792]{2,1,0:T(8,128)}, f32[3,32,1792]{2,1,0:T(8,128)}, f32[3,16,32]{2,1,0:T(8,128)}) custom-call(s32[1]{0:T(128)} %bitcast.ids.refs_0_, f32[3,16,32]{2,1,0:T(8,128)S(1)} %bitcast.7, f32[392,128]{1,0:T(8,128)S(1)} %choose.1.refs_2_, f32[392,128]{1,0:T(8,128)S(1)} %collective-permute-done.1.refs_3_, ...), custom_call_target="tpu_custom_call" | custom-call | tf_op jit(solution)/shard_map/final/pallas_call | solution.py:333
  (6 shorter events, 0.1 us)
Async XLA Ops:
  2.0 10.4 %collective-permute-start = (f32[16,48,128]{2,1,0:T(8,128)S(1)}, f32[16,48,128]{2,1,0:T(8,128)S(1)}, u32[]{:S(2)}, u32[]{:S(2)}) collective-permute-start(f32[16,48,128]{2,1,0:T(8,128)S(1)} %get-tuple-element.16), channel_id=1, source_target_pairs={{0,16},{16,0},{32,48},{48,32},{64,80},{80,64},{96,112},{112,96},{1... | collective-permute-start | bytes 1179656 | tf_op jit(solution)/shard_map/ppermute | solution.py:242
  12.5 27.3 %copy-start.2 = (f32[3,32,16]{1,2,0:T(8,128)S(1)}, f32[3,32,16]{1,2,0:T(8,128)}, u32[]{:S(2)}) copy-start(f32[3,32,16]{1,2,0:T(8,128)} %param.9) | copy-start | bytes 18436
  54.5 30.5 %copy-start.1 = (f32[3,32,1792]{2,1,0:T(8,128)S(1)}, f32[3,32,1792]{2,1,0:T(8,128)}, u32[]{:S(2)}) copy-start(f32[3,32,1792]{2,1,0:T(8,128)} %refs_5_.1) | copy-start | bytes 2064388
  78.4 6.5 %copy-start = (bf16[3,32,1792]{2,1,0:T(8,128)(2,1)S(1)}, bf16[3,32,1792]{2,1,0:T(8,128)(2,1)}, u32[]{:S(2)}) copy-start(bf16[3,32,1792]{2,1,0:T(8,128)(2,1)} %refs_4_.1) | copy-start | bytes 1032196
  78.5 6.5 %collective-permute-start.1 = (f32[392,128]{1,0:T(8,128)S(1)}, f32[392,128]{1,0:T(8,128)S(1)}, u32[]{:S(2)}, u32[]{:S(2)}) collective-permute-start(f32[392,128]{1,0:T(8,128)S(1)} %choose.1.refs_2_), channel_id=1, source_target_pairs={{0,16},{16,0},{32,48},{48,32},{64,80},{80,64},{96,112},{112,96},{1... | collective-permute-start | bytes 602120 | tf_op jit(solution)/shard_map/ppermute | solution.py:242

commit v4 on v3

--- a/solution.py
+++ b/solution.py
@@ -137,14 +137,6 @@
     inner[...] = jnp.concatenate([whole[0:8], whole[8:16], half[0:8], half[8:16]], axis=1)
 
 
-def stacked(a, b):
-    a_top, a_mid, a_last = split(a)
-    b_top, b_mid, b_last = split(b)
-    a = jnp.concatenate([a_top, a_top, a_top, a_mid, a_mid, a_last], axis=1)
-    b = jnp.concatenate([b_top, b_mid, b_last, b_top, b_mid, b_top], axis=1)
-    return lax.dot_general(a, b, (((1,), (1,)), ((), ())), preferred_element_type=jnp.float32)
-
-
 def choose_kernel(ids, one, two, out):
     out[CHIPS * FROWS :] = jnp.sum(two[:, FROWS:GROWS], axis=0)
     for core, arrived in enumerate((one, two)):
@@ -176,7 +168,7 @@
         (jnp.where(first, mine, other), middle, jnp.where(first, other, mine))
     ):
         rows = jnp.concatenate([rows[:, 0:COLS], rows[:, COLS : 2 * COLS]], axis=0)
-        gram = stacked(qt[mat], rows)
+        gram = outer(qt[mat], rows)
         rest = jnp.zeros((RANK, BLOCK - PAIR), jnp.float32)
         table.append(jnp.concatenate([gram, rows, rest], axis=1))
     table = jnp.stack(table)
@@ -253,7 +245,8 @@
         for place in range(16)
     ]
     planes = [
-        [(2 * chip + 1 - line_core) * 16 + place for place in range(16)] for chip in range(CHIPS)
+        [(2 * chip + 1 - line_core) * 16 + (5 * slot) % 16 for slot in range(16)]
+        for chip in range(CHIPS)
     ]
     return lax.all_to_all(
         x, ("replica", "fsdp"), 0, 0, axis_index_groups=lines + planes, tiled=True

time: 88.8 us -> 88.5 us (level)
  no operation moved by 1% of the time
where the time goes in v4:
time: 88.5 us; the launch traced here: 88 us
  blocking collectives  64.9 us (73%)
  starting transfers between devices  14.4 us (16%)
  Pallas kernels  6.83 us (8%)
  waiting for transfers between devices  1.06 us (1%)
    all_to_all x2, blocking collectives, exchange_mixed(): lax.all_to_all(x, ('replica', 'fsdp'), 0, 0, axis_index_groups=lines + pl...  37.5 us
    all_to_all x1, blocking collectives, exchange_z(): lax.all_to_all(x, 'replica', 0, 0, axis_index_groups=groups, tiled=True)  27.3 us
    ppermute x2, starting transfers between devices, sibling(): return lax.ppermute(x, 'replica', [(i, i ^ 1) for i in range(2 * CHIPS)])  14.4 us
    pallas_call x1, Pallas kernels, local(): pl.pallas_call(lambda *refs: final_kernel(lax.axis_size('replica'), *refs...  3.37 us
  transfers between devices with their start and end apart: 2, of which 1 were waited for; matrix products, arithmetic and copies ran while one was open for 0% of the time, Pallas kernels for 2%

profile of v4, /device:TPU:1, one launch (start us, length us, event | category | flops | bytes accessed | tf_op | source)
XLA Modules:
  0.0 88.0 jit_solution(5485983451406360160)
XLA Ops:
  0.6 1.4 %pack_send.1 = (f32[16,48,128]{2,1,0:T(8,128)S(1)}, s32[1]{0:T(128)S(4)}) custom-call(s32[1]{0:T(128)} %bitcast.ids.refs_0_, bf16[3,32,1792]{2,1,0:T(8,128)(2,1)} %refs_4_.1, bf16[3,32,1792]{2,1,0:T(8,128)(2,1)} %bitcast.10, f32[3,32,1792]{2,1,0:T(8,128)} %bitcast.8), custom_call_target="tpu_custom_call" | custom-call | tf_op jit(solution)/shard_map/pack_send/pallas_call | solution.py:261
  2.0 8.8 %collective-permute-start = (f32[16,48,128]{2,1,0:T(8,128)S(1)}, f32[16,48,128]{2,1,0:T(8,128)S(1)}, u32[]{:S(2)}, u32[]{:S(2)}) collective-permute-start(f32[16,48,128]{2,1,0:T(8,128)S(1)} %get-tuple-element.16), channel_id=1, source_target_pairs={{0,16},{16,0},{32,48},{48,32},{64,80},{80,64},{96,112},{112,96},{1... | collective-permute-start | bytes 1179656 | tf_op jit(solution)/shard_map/ppermute | solution.py:234
  10.8 1.6 %pack_keep.1 = (f32[16,48,128]{2,1,0:T(8,128)S(1)}, f32[3,32,1792]{2,1,0:T(8,128)S(1)}) custom-call(s32[1]{0:T(128)S(4)} %get-tuple-element.14.ids, bf16[3,32,1792]{2,1,0:T(8,128)(2,1)} %refs_4_.1, bf16[3,32,1792]{2,1,0:T(8,128)(2,1)} %bitcast.11, f32[3,32,1792]{2,1,0:T(8,128)} %bitcast.9), custom_call_target="tpu_custom_call" | custom-call | flops 1000000 | bytes 4000000 | tf_op jit(solution)/shard_map/pack_keep/pallas_call | solution.py:276
  12.4 0.0 collective-permute-done
  12.5 0.0 copy-start.2
  12.5 27.3 %all_to_all.15.got = f32[16,48,128]{2,1,0:T(8,128)S(1)} all-to-all(f32[16,48,128]{2,1,0:T(8,128)S(1)} %add.3), channel_id=1, replica_groups={{96,256,416,64,224,384,32,192,352,0,160,320,480,128,288,448},{368,16,17..., dimensions={0} | all-to-all | bytes 786432 | tf_op jit(solution)/shard_map/all_to_all | solution.py:239
  39.8 0.0 copy-done.2
  39.8 0.4 factor.1
  40.3 0.1 broadcast_in_dim.9
  40.3 13.8 %all_to_all.16.one = f32[16,32,128]{2,1,0:T(8,128)S(1)} all-to-all(f32[16,32,128]{2,1,0:T(8,128)S(1)} %broadcast_in_dim.9), channel_id=1, replica_groups={{0,288,64,352,128,416,192,480,256,32,320,96,384,160,448,224},{1,289,65,..., dimensions={0} | all-to-all | bytes 524288 | tf_op jit(solution)/shard_map/all_to_all | solution.py:251
  54.2 0.0 copy-start.1
  54.2 23.8 %all_to_all.17.two = f32[16,32,128]{2,1,0:T(8,128)S(1)} all-to-all(f32[16,32,128]{2,1,0:T(8,128)S(1)} %broadcast_in_dim.10), channel_id=1, replica_groups={{16,304,80,368,144,432,208,496,272,48,336,112,400,176,464,240},{17,305,..., dimensions={0} | all-to-all | bytes 524288 | tf_op jit(solution)/shard_map/all_to_all | solution.py:251
  77.9 0.0 copy-start
  78.0 5.6 %collective-permute-start.1 = (f32[392,128]{1,0:T(8,128)S(1)}, f32[392,128]{1,0:T(8,128)S(1)}, u32[]{:S(2)}, u32[]{:S(2)}) collective-permute-start(f32[392,128]{1,0:T(8,128)S(1)} %choose.1.refs_2_), channel_id=1, source_target_pairs={{0,16},{16,0},{32,48},{48,32},{64,80},{80,64},{96,112},{112,96},{1... | collective-permute-start | bytes 602120 | tf_op jit(solution)/shard_map/ppermute | solution.py:234
  83.6 1.1 %collective-permute-done.1.refs_3_ = f32[392,128]{1,0:T(8,128)S(1)} collective-permute-done((f32[392,128]{1,0:T(8,128)S(1)}, f32[392,128]{1,0:T(8,128)S(1)}, u32[]{:S(2)}, u32[]{:S(2)}) %collective-permute-start.1) | collective-permute-done | bytes 200736 | tf_op jit(solution)/shard_map/ppermute | solution.py:234
  84.6 0.0 copy-done.1
  84.6 0.0 copy-done
  84.6 3.4 %final.1 = (bf16[3,32,1792]{2,1,0:T(8,128)(2,1)}, f32[3,32,1792]{2,1,0:T(8,128)}, f32[3,32,1792]{2,1,0:T(8,128)}, f32[3,16,32]{2,1,0:T(8,128)}) custom-call(s32[1]{0:T(128)} %bitcast.ids.refs_0_, f32[3,16,32]{2,1,0:T(8,128)S(1)} %bitcast.7, f32[392,128]{1,0:T(8,128)S(1)} %choose.1.refs_2_, f32[392,128]{1,0:T(8,128)S(1)} %collective-permute-done.1.refs_3_, ...), custom_call_target="tpu_custom_call" | custom-call | tf_op jit(solution)/shard_map/final/pallas_call | solution.py:326
  (6 shorter events, 0.1 us)
Async XLA Ops:
  2.0 10.4 %collective-permute-start = (f32[16,48,128]{2,1,0:T(8,128)S(1)}, f32[16,48,128]{2,1,0:T(8,128)S(1)}, u32[]{:S(2)}, u32[]{:S(2)}) collective-permute-start(f32[16,48,128]{2,1,0:T(8,128)S(1)} %get-tuple-element.16), channel_id=1, source_target_pairs={{0,16},{16,0},{32,48},{48,32},{64,80},{80,64},{96,112},{112,96},{1... | collective-permute-start | bytes 1179656 | tf_op jit(solution)/shard_map/ppermute | solution.py:234
  12.5 27.3 %copy-start.2 = (f32[3,32,16]{1,2,0:T(8,128)S(1)}, f32[3,32,16]{1,2,0:T(8,128)}, u32[]{:S(2)}) copy-start(f32[3,32,16]{1,2,0:T(8,128)} %param.9) | copy-start | bytes 18436
  54.2 30.5 %copy-start.1 = (f32[3,32,1792]{2,1,0:T(8,128)S(1)}, f32[3,32,1792]{2,1,0:T(8,128)}, u32[]{:S(2)}) copy-start(f32[3,32,1792]{2,1,0:T(8,128)} %refs_5_.1) | copy-start | bytes 2064388
  77.9 6.7 %copy-start = (bf16[3,32,1792]{2,1,0:T(8,128)(2,1)S(1)}, bf16[3,32,1792]{2,1,0:T(8,128)(2,1)}, u32[]{:S(2)}) copy-start(bf16[3,32,1792]{2,1,0:T(8,128)(2,1)} %refs_4_.1) | copy-start | bytes 1032196
  78.0 6.6 %collective-permute-start.1 = (f32[392,128]{1,0:T(8,128)S(1)}, f32[392,128]{1,0:T(8,128)S(1)}, u32[]{:S(2)}, u32[]{:S(2)}) collective-permute-start(f32[392,128]{1,0:T(8,128)S(1)} %choose.1.refs_2_), channel_id=1, source_target_pairs={{0,16},{16,0},{32,48},{48,32},{64,80},{80,64},{96,112},{112,96},{1... | collective-permute-start | bytes 602120 | tf_op jit(solution)/shard_map/ppermute | solution.py:234

commit v5 on v4

--- a/solution.py
+++ b/solution.py
@@ -35,7 +35,11 @@
 
 
 def gather_slot(chip):
-    return (9 * chip) % CHIPS
+    return 2 * (chip & 7) + (chip >> 3)
+
+
+def gather_chip(slot):
+    return (slot >> 1) + 8 * (slot & 1)
 
 
 def swap_sides(x):
@@ -241,7 +245,7 @@
 
 def exchange_mixed(x, line_core):
     lines = [
-        [(2 * gather_slot(slot) + line_core) * 16 + place for slot in range(CHIPS)]
+        [(2 * gather_chip(slot) + line_core) * 16 + place for slot in range(CHIPS)]
         for place in range(16)
     ]
     planes = [

time: 88.5 us -> 90.8 us (1.026)
  blocking collectives: 64.9 us -> 66.8 us
    all_to_all x2, blocking collectives: 37.5 us -> 39.5 us  [exchange_mixed(): lax.all_to_all(x, ('replica', 'fsdp'), 0, 0, axis_index_groups=lines + pl...]
where the time goes in v5:
time: 90.8 us; the launch traced here: 90.4 us
  blocking collectives  66.8 us (74%)
  starting transfers between devices  14.8 us (16%)
  Pallas kernels  6.83 us (8%)
  waiting for transfers between devices  1.06 us (1%)
    all_to_all x2, blocking collectives, exchange_mixed(): lax.all_to_all(x, ('replica', 'fsdp'), 0, 0, axis_index_groups=lines + pl...  39.5 us
    all_to_all x1, blocking collectives, exchange_z(): lax.all_to_all(x, 'replica', 0, 0, axis_index_groups=groups, tiled=True)  27.3 us
    ppermute x2, starting transfers between devices, sibling(): return lax.ppermute(x, 'replica', [(i, i ^ 1) for i in range(2 * CHIPS)])  14.8 us
    pallas_call x1, Pallas kernels, local(): pl.pallas_call(lambda *refs: final_kernel(lax.axis_size('replica'), *refs...  3.37 us
  transfers between devices with their start and end apart: 2, of which 1 were waited for; matrix products, arithmetic and copies ran while one was open for 0% of the time, Pallas kernels for 2%

profile of v5, /device:TPU:1, one launch (start us, length us, event | category | flops | bytes accessed | tf_op | source)
XLA Modules:
  0.0 90.4 jit_solution(6969046952003115060)
XLA Ops:
  0.6 1.4 %pack_send.1 = (f32[16,48,128]{2,1,0:T(8,128)S(1)}, s32[1]{0:T(128)S(4)}) custom-call(s32[1]{0:T(128)} %bitcast.ids.refs_0_, bf16[3,32,1792]{2,1,0:T(8,128)(2,1)} %refs_4_.1, bf16[3,32,1792]{2,1,0:T(8,128)(2,1)} %bitcast.10, f32[3,32,1792]{2,1,0:T(8,128)} %bitcast.8), custom_call_target="tpu_custom_call" | custom-call | tf_op jit(solution)/shard_map/pack_send/pallas_call | solution.py:265
  2.0 8.8 %collective-permute-start = (f32[16,48,128]{2,1,0:T(8,128)S(1)}, f32[16,48,128]{2,1,0:T(8,128)S(1)}, u32[]{:S(2)}, u32[]{:S(2)}) collective-permute-start(f32[16,48,128]{2,1,0:T(8,128)S(1)} %get-tuple-element.16), channel_id=1, source_target_pairs={{0,16},{16,0},{32,48},{48,32},{64,80},{80,64},{96,112},{112,96},{1... | collective-permute-start | bytes 1179656 | tf_op jit(solution)/shard_map/ppermute | solution.py:238
  10.8 1.6 %pack_keep.1 = (f32[16,48,128]{2,1,0:T(8,128)S(1)}, f32[3,32,1792]{2,1,0:T(8,128)S(1)}) custom-call(s32[1]{0:T(128)S(4)} %get-tuple-element.14.ids, bf16[3,32,1792]{2,1,0:T(8,128)(2,1)} %refs_4_.1, bf16[3,32,1792]{2,1,0:T(8,128)(2,1)} %bitcast.11, f32[3,32,1792]{2,1,0:T(8,128)} %bitcast.9), custom_call_target="tpu_custom_call" | custom-call | flops 1000000 | bytes 4000000 | tf_op jit(solution)/shard_map/pack_keep/pallas_call | solution.py:280
  12.4 0.0 collective-permute-done
  12.5 0.0 copy-start.2
  12.5 27.3 %all_to_all.15.got = f32[16,48,128]{2,1,0:T(8,128)S(1)} all-to-all(f32[16,48,128]{2,1,0:T(8,128)S(1)} %add.3), channel_id=1, replica_groups={{96,256,416,64,224,384,32,192,352,0,160,320,480,128,288,448},{368,16,17..., dimensions={0} | all-to-all | bytes 786432 | tf_op jit(solution)/shard_map/all_to_all | solution.py:243
  39.8 0.0 copy-done.2
  39.8 0.4 factor.1
  40.3 0.1 broadcast_in_dim.9
  40.3 13.8 %all_to_all.16.one = f32[16,32,128]{2,1,0:T(8,128)S(1)} all-to-all(f32[16,32,128]{2,1,0:T(8,128)S(1)} %broadcast_in_dim.9), channel_id=1, replica_groups={{0,256,32,288,64,320,96,352,128,384,160,416,192,448,224,480},{1,257,33,..., dimensions={0} | all-to-all | bytes 524288 | tf_op jit(solution)/shard_map/all_to_all | solution.py:255
  54.2 0.0 copy-start.1
  54.2 25.7 %all_to_all.17.two = f32[16,32,128]{2,1,0:T(8,128)S(1)} all-to-all(f32[16,32,128]{2,1,0:T(8,128)S(1)} %broadcast_in_dim.10), channel_id=1, replica_groups={{16,272,48,304,80,336,112,368,144,400,176,432,208,464,240,496},{17,273,..., dimensions={0} | all-to-all | bytes 524288 | tf_op jit(solution)/shard_map/all_to_all | solution.py:255
  79.9 0.0 copy-start
  80.0 6.0 %collective-permute-start.1 = (f32[392,128]{1,0:T(8,128)S(1)}, f32[392,128]{1,0:T(8,128)S(1)}, u32[]{:S(2)}, u32[]{:S(2)}) collective-permute-start(f32[392,128]{1,0:T(8,128)S(1)} %choose.1.refs_2_), channel_id=1, source_target_pairs={{0,16},{16,0},{32,48},{48,32},{64,80},{80,64},{96,112},{112,96},{1... | collective-permute-start | bytes 602120 | tf_op jit(solution)/shard_map/ppermute | solution.py:238
  86.0 1.1 %collective-permute-done.1.refs_3_ = f32[392,128]{1,0:T(8,128)S(1)} collective-permute-done((f32[392,128]{1,0:T(8,128)S(1)}, f32[392,128]{1,0:T(8,128)S(1)}, u32[]{:S(2)}, u32[]{:S(2)}) %collective-permute-start.1) | collective-permute-done | bytes 200736 | tf_op jit(solution)/shard_map/ppermute | solution.py:238
  87.1 0.0 copy-done.1
  87.1 0.0 copy-done
  87.1 3.4 %final.1 = (bf16[3,32,1792]{2,1,0:T(8,128)(2,1)}, f32[3,32,1792]{2,1,0:T(8,128)}, f32[3,32,1792]{2,1,0:T(8,128)}, f32[3,16,32]{2,1,0:T(8,128)}) custom-call(s32[1]{0:T(128)} %bitcast.ids.refs_0_, f32[3,16,32]{2,1,0:T(8,128)S(1)} %bitcast.7, f32[392,128]{1,0:T(8,128)S(1)} %choose.1.refs_2_, f32[392,128]{1,0:T(8,128)S(1)} %collective-permute-done.1.refs_3_, ...), custom_call_target="tpu_custom_call" | custom-call | tf_op jit(solution)/shard_map/final/pallas_call | solution.py:330
  (6 shorter events, 0.1 us)
Async XLA Ops:
  2.0 10.4 %collective-permute-start = (f32[16,48,128]{2,1,0:T(8,128)S(1)}, f32[16,48,128]{2,1,0:T(8,128)S(1)}, u32[]{:S(2)}, u32[]{:S(2)}) collective-permute-start(f32[16,48,128]{2,1,0:T(8,128)S(1)} %get-tuple-element.16), channel_id=1, source_target_pairs={{0,16},{16,0},{32,48},{48,32},{64,80},{80,64},{96,112},{112,96},{1... | collective-permute-start | bytes 1179656 | tf_op jit(solution)/shard_map/ppermute | solution.py:238
  12.5 27.3 %copy-start.2 = (f32[3,32,16]{1,2,0:T(8,128)S(1)}, f32[3,32,16]{1,2,0:T(8,128)}, u32[]{:S(2)}) copy-start(f32[3,32,16]{1,2,0:T(8,128)} %param.9) | copy-start | bytes 18436
  54.2 32.9 %copy-start.1 = (f32[3,32,1792]{2,1,0:T(8,128)S(1)}, f32[3,32,1792]{2,1,0:T(8,128)}, u32[]{:S(2)}) copy-start(f32[3,32,1792]{2,1,0:T(8,128)} %refs_5_.1) | copy-start | bytes 2064388
  79.9 7.1 %copy-start = (bf16[3,32,1792]{2,1,0:T(8,128)(2,1)S(1)}, bf16[3,32,1792]{2,1,0:T(8,128)(2,1)}, u32[]{:S(2)}) copy-start(bf16[3,32,1792]{2,1,0:T(8,128)(2,1)} %refs_4_.1) | copy-start | bytes 1032196
  80.0 7.1 %collective-permute-start.1 = (f32[392,128]{1,0:T(8,128)S(1)}, f32[392,128]{1,0:T(8,128)S(1)}, u32[]{:S(2)}, u32[]{:S(2)}) collective-permute-start(f32[392,128]{1,0:T(8,128)S(1)} %choose.1.refs_2_), channel_id=1, source_target_pairs={{0,16},{16,0},{32,48},{48,32},{64,80},{80,64},{96,112},{112,96},{1... | collective-permute-start | bytes 602120 | tf_op jit(solution)/shard_map/ppermute | solution.py:238

commit v6 on v4

--- a/solution.py
+++ b/solution.py
@@ -27,11 +27,11 @@
 
 
 def slot_of(chip, core):
-    return ((13 * (chip - 3)) & 15) ^ (8 * core)
+    return ((3 * (chip - 13)) & 15) ^ (8 * core)
 
 
 def chip_at(slot, core):
-    return (3 + 8 * core + 5 * slot) % CHIPS
+    return (13 + 8 * core + 11 * slot) % CHIPS
 
 
 def gather_slot(chip):

time: 88.5 us -> 87.7 us (level)
  starting transfers between devices: 14.4 us -> 13.1 us
    all_to_all x1, blocking collectives: 27.3 us -> 29.5 us  [exchange_z(): lax.all_to_all(x, 'replica', 0, 0, axis_index_groups=groups, tiled=True)]
    all_to_all x2, blocking collectives: 37.5 us -> 35.8 us  [exchange_mixed(): lax.all_to_all(x, ('replica', 'fsdp'), 0, 0, axis_index_groups=lines + pl...]
    ppermute x2, starting transfers between devices: 14.4 us -> 13.1 us  [sibling(): return lax.ppermute(x, 'replica', [(i, i ^ 1) for i in range(2 * CHIPS)])]
where the time goes in v6:
time: 87.7 us; the launch traced here: 87.3 us
  blocking collectives  65.4 us (75%)
  starting transfers between devices  13.1 us (15%)
  Pallas kernels  6.83 us (8%)
  waiting for transfers between devices  1.06 us (1%)
    all_to_all x2, blocking collectives, exchange_mixed(): lax.all_to_all(x, ('replica', 'fsdp'), 0, 0, axis_index_groups=lines + pl...  35.8 us
    all_to_all x1, blocking collectives, exchange_z(): lax.all_to_all(x, 'replica', 0, 0, axis_index_groups=groups, tiled=True)  29.5 us
    ppermute x2, starting transfers between devices, sibling(): return lax.ppermute(x, 'replica', [(i, i ^ 1) for i in range(2 * CHIPS)])  13.1 us
    pallas_call x1, Pallas kernels, local(): pl.pallas_call(lambda *refs: final_kernel(lax.axis_size('replica'), *refs...  3.37 us
  transfers between devices with their start and end apart: 2, of which 1 were waited for; matrix products, arithmetic and copies ran while one was open for 0% of the time, Pallas kernels for 2%

profile of v6, /device:TPU:1, one launch (start us, length us, event | category | flops | bytes accessed | tf_op | source)
XLA Modules:
  0.0 87.3 jit_solution(14455627689099491754)
XLA Ops:
  0.6 1.4 %pack_send.1 = (f32[16,48,128]{2,1,0:T(8,128)S(1)}, s32[1]{0:T(128)S(4)}) custom-call(s32[1]{0:T(128)} %bitcast.ids.refs_0_, bf16[3,32,1792]{2,1,0:T(8,128)(2,1)} %refs_4_.1, bf16[3,32,1792]{2,1,0:T(8,128)(2,1)} %bitcast.10, f32[3,32,1792]{2,1,0:T(8,128)} %bitcast.8), custom_call_target="tpu_custom_call" | custom-call | tf_op jit(solution)/shard_map/pack_send/pallas_call | solution.py:261
  2.0 8.8 %collective-permute-start = (f32[16,48,128]{2,1,0:T(8,128)S(1)}, f32[16,48,128]{2,1,0:T(8,128)S(1)}, u32[]{:S(2)}, u32[]{:S(2)}) collective-permute-start(f32[16,48,128]{2,1,0:T(8,128)S(1)} %get-tuple-element.16), channel_id=1, source_target_pairs={{0,16},{16,0},{32,48},{48,32},{64,80},{80,64},{96,112},{112,96},{1... | collective-permute-start | bytes 1179656 | tf_op jit(solution)/shard_map/ppermute | solution.py:234
  10.8 1.6 %pack_keep.1 = (f32[16,48,128]{2,1,0:T(8,128)S(1)}, f32[3,32,1792]{2,1,0:T(8,128)S(1)}) custom-call(s32[1]{0:T(128)S(4)} %get-tuple-element.14.ids, bf16[3,32,1792]{2,1,0:T(8,128)(2,1)} %refs_4_.1, bf16[3,32,1792]{2,1,0:T(8,128)(2,1)} %bitcast.11, f32[3,32,1792]{2,1,0:T(8,128)} %bitcast.9), custom_call_target="tpu_custom_call" | custom-call | flops 1000000 | bytes 4000000 | tf_op jit(solution)/shard_map/pack_keep/pallas_call | solution.py:276
  12.4 0.0 collective-permute-done
  12.5 0.0 copy-start.2
  12.5 29.5 %all_to_all.15.got = f32[16,48,128]{2,1,0:T(8,128)S(1)} all-to-all(f32[16,48,128]{2,1,0:T(8,128)S(1)} %add.3), channel_id=1, replica_groups={{416,256,96,448,288,128,480,320,160,0,352,192,32,384,224,64},{176,16,36..., dimensions={0} | all-to-all | bytes 786432 | tf_op jit(solution)/shard_map/all_to_all | solution.py:239
  42.0 0.0 copy-done.2
  42.0 0.4 factor.1
  42.5 0.1 broadcast_in_dim.9
  42.5 13.8 %all_to_all.16.one = f32[16,32,128]{2,1,0:T(8,128)S(1)} all-to-all(f32[16,32,128]{2,1,0:T(8,128)S(1)} %broadcast_in_dim.9), channel_id=1, replica_groups={{0,288,64,352,128,416,192,480,256,32,320,96,384,160,448,224},{1,289,65,..., dimensions={0} | all-to-all | bytes 524288 | tf_op jit(solution)/shard_map/all_to_all | solution.py:251
  56.4 0.0 copy-start.1
  56.4 22.1 %all_to_all.17.two = f32[16,32,128]{2,1,0:T(8,128)S(1)} all-to-all(f32[16,32,128]{2,1,0:T(8,128)S(1)} %broadcast_in_dim.10), channel_id=1, replica_groups={{16,304,80,368,144,432,208,496,272,48,336,112,400,176,464,240},{17,305,..., dimensions={0} | all-to-all | bytes 524288 | tf_op jit(solution)/shard_map/all_to_all | solution.py:251
  78.5 0.0 copy-start
  78.5 4.3 %collective-permute-start.1 = (f32[392,128]{1,0:T(8,128)S(1)}, f32[392,128]{1,0:T(8,128)S(1)}, u32[]{:S(2)}, u32[]{:S(2)}) collective-permute-start(f32[392,128]{1,0:T(8,128)S(1)} %choose.1.refs_2_), channel_id=1, source_target_pairs={{0,16},{16,0},{32,48},{48,32},{64,80},{80,64},{96,112},{112,96},{1... | collective-permute-start | bytes 602120 | tf_op jit(solution)/shard_map/ppermute | solution.py:234
  82.8 1.1 %collective-permute-done.1.refs_3_ = f32[392,128]{1,0:T(8,128)S(1)} collective-permute-done((f32[392,128]{1,0:T(8,128)S(1)}, f32[392,128]{1,0:T(8,128)S(1)}, u32[]{:S(2)}, u32[]{:S(2)}) %collective-permute-start.1) | collective-permute-done | bytes 200736 | tf_op jit(solution)/shard_map/ppermute | solution.py:234
  83.9 0.0 copy-done.1
  83.9 0.0 copy-done
  83.9 3.4 %final.1 = (bf16[3,32,1792]{2,1,0:T(8,128)(2,1)}, f32[3,32,1792]{2,1,0:T(8,128)}, f32[3,32,1792]{2,1,0:T(8,128)}, f32[3,16,32]{2,1,0:T(8,128)}) custom-call(s32[1]{0:T(128)} %bitcast.ids.refs_0_, f32[3,16,32]{2,1,0:T(8,128)S(1)} %bitcast.7, f32[392,128]{1,0:T(8,128)S(1)} %choose.1.refs_2_, f32[392,128]{1,0:T(8,128)S(1)} %collective-permute-done.1.refs_3_, ...), custom_call_target="tpu_custom_call" | custom-call | tf_op jit(solution)/shard_map/final/pallas_call | solution.py:326
  (6 shorter events, 0.1 us)
Async XLA Ops:
  2.0 10.4 %collective-permute-start = (f32[16,48,128]{2,1,0:T(8,128)S(1)}, f32[16,48,128]{2,1,0:T(8,128)S(1)}, u32[]{:S(2)}, u32[]{:S(2)}) collective-permute-start(f32[16,48,128]{2,1,0:T(8,128)S(1)} %get-tuple-element.16), channel_id=1, source_target_pairs={{0,16},{16,0},{32,48},{48,32},{64,80},{80,64},{96,112},{112,96},{1... | collective-permute-start | bytes 1179656 | tf_op jit(solution)/shard_map/ppermute | solution.py:234
  12.5 29.5 %copy-start.2 = (f32[3,32,16]{1,2,0:T(8,128)S(1)}, f32[3,32,16]{1,2,0:T(8,128)}, u32[]{:S(2)}) copy-start(f32[3,32,16]{1,2,0:T(8,128)} %param.9) | copy-start | bytes 18436
  56.4 27.5 %copy-start.1 = (f32[3,32,1792]{2,1,0:T(8,128)S(1)}, f32[3,32,1792]{2,1,0:T(8,128)}, u32[]{:S(2)}) copy-start(f32[3,32,1792]{2,1,0:T(8,128)} %refs_5_.1) | copy-start | bytes 2064388
  78.5 5.4 %copy-start = (bf16[3,32,1792]{2,1,0:T(8,128)(2,1)S(1)}, bf16[3,32,1792]{2,1,0:T(8,128)(2,1)}, u32[]{:S(2)}) copy-start(bf16[3,32,1792]{2,1,0:T(8,128)(2,1)} %refs_4_.1) | copy-start | bytes 1032196
  78.5 5.4 %collective-permute-start.1 = (f32[392,128]{1,0:T(8,128)S(1)}, f32[392,128]{1,0:T(8,128)S(1)}, u32[]{:S(2)}, u32[]{:S(2)}) collective-permute-start(f32[392,128]{1,0:T(8,128)S(1)} %choose.1.refs_2_), channel_id=1, source_target_pairs={{0,16},{16,0},{32,48},{48,32},{64,80},{80,64},{96,112},{112,96},{1... | collective-permute-start | bytes 602120 | tf_op jit(solution)/shard_map/ppermute | solution.py:234

commit v7 on v6

--- a/solution.py
+++ b/solution.py
@@ -27,11 +27,11 @@
 
 
 def slot_of(chip, core):
-    return ((3 * (chip - 13)) & 15) ^ (8 * core)
+    return ((3 * (chip - 5)) & 15) ^ (8 * core)
 
 
 def chip_at(slot, core):
-    return (13 + 8 * core + 11 * slot) % CHIPS
+    return (5 + 8 * core + 11 * slot) % CHIPS
 
 
 def gather_slot(chip):

time: 87.7 us -> 89.1 us (1.016)
  starting transfers between devices: 13.1 us -> 15.2 us
    ppermute x2, starting transfers between devices: 13.1 us -> 15.2 us  [sibling(): return lax.ppermute(x, 'replica', [(i, i ^ 1) for i in range(2 * CHIPS)])]
where the time goes in v7:
time: 89.1 us; the launch traced here: 88.7 us
  blocking collectives  64.7 us (73%)
  starting transfers between devices  15.2 us (17%)
  Pallas kernels  6.83 us (8%)
  waiting for transfers between devices  1.06 us (1%)
    all_to_all x2, blocking collectives, exchange_mixed(): lax.all_to_all(x, ('replica', 'fsdp'), 0, 0, axis_index_groups=lines + pl...  35.3 us
    all_to_all x1, blocking collectives, exchange_z(): lax.all_to_all(x, 'replica', 0, 0, axis_index_groups=groups, tiled=True)  29.4 us
    ppermute x2, starting transfers between devices, sibling(): return lax.ppermute(x, 'replica', [(i, i ^ 1) for i in range(2 * CHIPS)])  15.2 us
    pallas_call x1, Pallas kernels, local(): pl.pallas_call(lambda *refs: final_kernel(lax.axis_size('replica'), *refs...  3.37 us
  transfers between devices with their start and end apart: 2, of which 1 were waited for; matrix products, arithmetic and copies ran while one was open for 0% of the time, Pallas kernels for 2%

profile of v7, /device:TPU:1, one launch (start us, length us, event | category | flops | bytes accessed | tf_op | source)
XLA Modules:
  0.0 88.7 jit_solution(2683937732170607551)
XLA Ops:
  0.6 1.4 %pack_send.1 = (f32[16,48,128]{2,1,0:T(8,128)S(1)}, s32[1]{0:T(128)S(4)}) custom-call(s32[1]{0:T(128)} %bitcast.ids.refs_0_, bf16[3,32,1792]{2,1,0:T(8,128)(2,1)} %refs_4_.1, bf16[3,32,1792]{2,1,0:T(8,128)(2,1)} %bitcast.10, f32[3,32,1792]{2,1,0:T(8,128)} %bitcast.8), custom_call_target="tpu_custom_call" | custom-call | tf_op jit(solution)/shard_map/pack_send/pallas_call | solution.py:261
  2.0 8.8 %collective-permute-start = (f32[16,48,128]{2,1,0:T(8,128)S(1)}, f32[16,48,128]{2,1,0:T(8,128)S(1)}, u32[]{:S(2)}, u32[]{:S(2)}) collective-permute-start(f32[16,48,128]{2,1,0:T(8,128)S(1)} %get-tuple-element.16), channel_id=1, source_target_pairs={{0,16},{16,0},{32,48},{48,32},{64,80},{80,64},{96,112},{112,96},{1... | collective-permute-start | bytes 1179656 | tf_op jit(solution)/shard_map/ppermute | solution.py:234
  10.8 1.6 %pack_keep.1 = (f32[16,48,128]{2,1,0:T(8,128)S(1)}, f32[3,32,1792]{2,1,0:T(8,128)S(1)}) custom-call(s32[1]{0:T(128)S(4)} %get-tuple-element.14.ids, bf16[3,32,1792]{2,1,0:T(8,128)(2,1)} %refs_4_.1, bf16[3,32,1792]{2,1,0:T(8,128)(2,1)} %bitcast.11, f32[3,32,1792]{2,1,0:T(8,128)} %bitcast.9), custom_call_target="tpu_custom_call" | custom-call | flops 1000000 | bytes 4000000 | tf_op jit(solution)/shard_map/pack_keep/pallas_call | solution.py:276
  12.4 0.0 collective-permute-done
  12.5 0.0 copy-start.2
  12.5 29.4 %all_to_all.15.got = f32[16,48,128]{2,1,0:T(8,128)S(1)} all-to-all(f32[16,48,128]{2,1,0:T(8,128)S(1)} %add.3), channel_id=1, replica_groups={{160,0,352,192,32,384,224,64,416,256,96,448,288,128,480,320},{432,272,1..., dimensions={0} | all-to-all | bytes 786432 | tf_op jit(solution)/shard_map/all_to_all | solution.py:239
  41.9 0.0 copy-done.2
  41.9 0.4 factor.1
  42.4 0.1 broadcast_in_dim.9
  42.4 13.8 %all_to_all.16.one = f32[16,32,128]{2,1,0:T(8,128)S(1)} all-to-all(f32[16,32,128]{2,1,0:T(8,128)S(1)} %broadcast_in_dim.9), channel_id=1, replica_groups={{0,288,64,352,128,416,192,480,256,32,320,96,384,160,448,224},{1,289,65,..., dimensions={0} | all-to-all | bytes 524288 | tf_op jit(solution)/shard_map/all_to_all | solution.py:251
  56.3 0.0 copy-start.1
  56.3 21.5 %all_to_all.17.two = f32[16,32,128]{2,1,0:T(8,128)S(1)} all-to-all(f32[16,32,128]{2,1,0:T(8,128)S(1)} %broadcast_in_dim.10), channel_id=1, replica_groups={{16,304,80,368,144,432,208,496,272,48,336,112,400,176,464,240},{17,305,..., dimensions={0} | all-to-all | bytes 524288 | tf_op jit(solution)/shard_map/all_to_all | solution.py:251
  77.8 0.0 copy-start
  77.9 6.4 %collective-permute-start.1 = (f32[392,128]{1,0:T(8,128)S(1)}, f32[392,128]{1,0:T(8,128)S(1)}, u32[]{:S(2)}, u32[]{:S(2)}) collective-permute-start(f32[392,128]{1,0:T(8,128)S(1)} %choose.1.refs_2_), channel_id=1, source_target_pairs={{0,16},{16,0},{32,48},{48,32},{64,80},{80,64},{96,112},{112,96},{1... | collective-permute-start | bytes 602120 | tf_op jit(solution)/shard_map/ppermute | solution.py:234
  84.3 1.1 %collective-permute-done.1.refs_3_ = f32[392,128]{1,0:T(8,128)S(1)} collective-permute-done((f32[392,128]{1,0:T(8,128)S(1)}, f32[392,128]{1,0:T(8,128)S(1)}, u32[]{:S(2)}, u32[]{:S(2)}) %collective-permute-start.1) | collective-permute-done | bytes 200736 | tf_op jit(solution)/shard_map/ppermute | solution.py:234
  85.3 0.0 copy-done.1
  85.3 0.0 copy-done
  85.3 3.4 %final.1 = (bf16[3,32,1792]{2,1,0:T(8,128)(2,1)}, f32[3,32,1792]{2,1,0:T(8,128)}, f32[3,32,1792]{2,1,0:T(8,128)}, f32[3,16,32]{2,1,0:T(8,128)}) custom-call(s32[1]{0:T(128)} %bitcast.ids.refs_0_, f32[3,16,32]{2,1,0:T(8,128)S(1)} %bitcast.7, f32[392,128]{1,0:T(8,128)S(1)} %choose.1.refs_2_, f32[392,128]{1,0:T(8,128)S(1)} %collective-permute-done.1.refs_3_, ...), custom_call_target="tpu_custom_call" | custom-call | tf_op jit(solution)/shard_map/final/pallas_call | solution.py:326
  (6 shorter events, 0.1 us)
Async XLA Ops:
  2.0 10.4 %collective-permute-start = (f32[16,48,128]{2,1,0:T(8,128)S(1)}, f32[16,48,128]{2,1,0:T(8,128)S(1)}, u32[]{:S(2)}, u32[]{:S(2)}) collective-permute-start(f32[16,48,128]{2,1,0:T(8,128)S(1)} %get-tuple-element.16), channel_id=1, source_target_pairs={{0,16},{16,0},{32,48},{48,32},{64,80},{80,64},{96,112},{112,96},{1... | collective-permute-start | bytes 1179656 | tf_op jit(solution)/shard_map/ppermute | solution.py:234
  12.5 29.4 %copy-start.2 = (f32[3,32,16]{1,2,0:T(8,128)S(1)}, f32[3,32,16]{1,2,0:T(8,128)}, u32[]{:S(2)}) copy-start(f32[3,32,16]{1,2,0:T(8,128)} %param.9) | copy-start | bytes 18436
  56.3 29.1 %copy-start.1 = (f32[3,32,1792]{2,1,0:T(8,128)S(1)}, f32[3,32,1792]{2,1,0:T(8,128)}, u32[]{:S(2)}) copy-start(f32[3,32,1792]{2,1,0:T(8,128)} %refs_5_.1) | copy-start | bytes 2064388
  77.8 7.5 %copy-start = (bf16[3,32,1792]{2,1,0:T(8,128)(2,1)S(1)}, bf16[3,32,1792]{2,1,0:T(8,128)(2,1)}, u32[]{:S(2)}) copy-start(bf16[3,32,1792]{2,1,0:T(8,128)(2,1)} %refs_4_.1) | copy-start | bytes 1032196
  77.9 7.5 %collective-permute-start.1 = (f32[392,128]{1,0:T(8,128)S(1)}, f32[392,128]{1,0:T(8,128)S(1)}, u32[]{:S(2)}, u32[]{:S(2)}) collective-permute-start(f32[392,128]{1,0:T(8,128)S(1)} %choose.1.refs_2_), channel_id=1, source_target_pairs={{0,16},{16,0},{32,48},{48,32},{64,80},{80,64},{96,112},{112,96},{1... | collective-permute-start | bytes 602120 | tf_op jit(solution)/shard_map/ppermute | solution.py:234
